TPU v7x, 256 devices: a whole 4x4x8 slice. The times are simulated.
256 devices in a mesh: section: 8 (over z_lo, y), ctx: 32 (over x, z_hi, core).
Axes of the slice: x: 4, y: 4, z: 8 (z_hi: 4, z_lo: 2; z = z_hi * 2 + z_lo), core: 2. Of those that a mesh axis runs over, the one named last changes fastest.
Arguments:
- layer_input: bfloat16 [8, 6144, 5120], P('section', 'ctx'), may hold values from -7 to 7
- self_q: bfloat16 [6144, 640], P('ctx'), may hold values from -10 to 10
- self_kv: bfloat16 [6144, 256], P('ctx'), may hold values from -10 to 10
- self_out_weight: bfloat16 [640, 5120], P(None, ('section', 'ctx')), may hold values from -0.25 to 0.25
- kv_weight: bfloat16 [5120, 256], P(('section', 'ctx')), may hold values from -0.078125 to 0.078125
- q_weight: bfloat16 [8, 5120, 640], P('section', 'ctx'), may hold values from -5 to 5
- out_weight: bfloat16 [8, 640, 5120], P('section', None, 'ctx'), may hold values from -0.25 to 0.25
Outputs:
- updates: bfloat16 [8, 6144, 5120], P('section', 'ctx')
- shared_kv: bfloat16 [6144, 256], P('ctx')
All inputs are finite; a program needn't handle non-finite values.
Results may differ from a plain program's by a relative error of at most 0.0247.
Values may be sent and summed in bfloat16 or wider, within the bound.
A program may use at most 128 MiB of HBM per device.

v0:
```python
import math

import jax
import jax.numpy as jnp
from jax import lax
from jax.sharding import PartitionSpec as P

WINDOW = 128


def shifted(value, axis, steps):
    count = lax.axis_size(axis)
    first, last = (max(0, -steps), min(count, count - steps))
    return lax.ppermute(value, axis, [(source, source + steps) for source in range(first, last)])


def attend_block(queries, keys, values, query_pos, key_pos, reach, factor):
    rows = queries.shape[0]
    head_size = keys.shape[1]
    heads = queries.shape[1] // head_size
    grouped = queries.reshape(rows, heads, head_size)
    scores = jnp.einsum("bhd,kd->hbk", grouped, keys, preferred_element_type=jnp.float32) * factor
    allowed = (
        (key_pos[None, :] <= query_pos[:, None])
        & (key_pos[None, :] > query_pos[:, None] - reach)
        & (key_pos[None, :] >= 0)
    )
    scores = jnp.where(allowed[None], scores, -1e30)
    top = jnp.max(scores, axis=-1, keepdims=True)
    expo = jnp.where(allowed[None], jnp.exp(scores - top), 0.0)
    numer = jnp.einsum(
        "hbk,kd->bhd", expo.astype(jnp.bfloat16), values, preferred_element_type=jnp.float32
    )
    denom = jnp.sum(expo, axis=-1).T
    return (numer / denom[:, :, None]).reshape(rows, heads * head_size).astype(jnp.bfloat16)


def online_step(state, block, positions, piece):
    top, total, accum = state
    rows = block.shape[0]
    head_size = piece.shape[1] // 2
    heads = block.shape[1] // head_size
    keys = piece[:, :head_size]
    values = piece[:, head_size:]
    key_pos = jnp.arange(piece.shape[0], dtype=jnp.int32)
    grouped = block.reshape(rows, heads, head_size)
    scores = jnp.einsum("bhd,kd->hbk", grouped, keys, preferred_element_type=jnp.float32)
    allowed = key_pos[None, :] <= positions[:, None]
    scores = jnp.where(allowed[None], scores, -1e30)
    new_top = jnp.maximum(top, jnp.max(scores, axis=-1))
    fade = jnp.exp(top - new_top)
    expo = jnp.where(allowed[None], jnp.exp(scores - new_top[:, :, None]), 0.0)
    total = jnp.sum(expo, axis=-1)
    accum = accum * fade.T[:, :, None] + jnp.einsum(
        "hbk,kd->bhd", expo.astype(jnp.bfloat16), values, preferred_element_type=jnp.float32
    )
    return (new_top, total, accum)


def rows_times(left, piece):
    return jnp.dot(left, piece, preferred_element_type=jnp.float32)


def contract_with(left, piece):
    return jnp.dot(left, piece, preferred_element_type=jnp.float32)


def per_device(layer_input, self_q, self_kv, self_out_weight, kv_weight, q_weight, out_weight):
    tok_rows = self_q.shape[0]
    head_size = self_kv.shape[1] // 2
    ctx_index = lax.axis_index("ctx")
    sections = lax.axis_size("section")
    factor = 1.0 / math.sqrt(head_size)
    rim = shifted(self_kv, "ctx", 1)
    near = jnp.concatenate([rim, self_kv], axis=0)
    base = ctx_index * tok_rows
    near_pos = base - tok_rows + jnp.arange(2 * tok_rows, dtype=jnp.int32)
    share = tok_rows // sections
    first = lax.axis_index("section") * share
    own_queries = lax.dynamic_slice_in_dim(self_q, first, share, 0)
    query_pos = base + first + jnp.arange(share, dtype=jnp.int32)
    window_out = attend_block(
        own_queries, near[:, :head_size], near[:, head_size:], query_pos, near_pos, WINDOW, factor
    )
    mixed = rows_times(
        window_out, lax.all_gather(self_out_weight, ("section", "ctx"), axis=1, tiled=True)
    ).astype(jnp.bfloat16)
    wide = mixed.astype(jnp.float32)
    squares = jnp.sum(wide * wide, axis=-1, keepdims=True)
    raw = contract_with(mixed, lax.all_gather(kv_weight, ("section", "ctx"), axis=0, tiled=True))
    part_rows = (raw * lax.rsqrt(squares / mixed.shape[1] + 1e-06)).astype(jnp.bfloat16)
    shared = lax.all_gather(part_rows, "section", axis=0, tiled=True)
    hidden = layer_input[0]
    wide_hidden = hidden.astype(jnp.float32)
    normed = (
        wide_hidden * lax.rsqrt(jnp.mean(wide_hidden * wide_hidden, axis=-1, keepdims=True) + 1e-06)
    ).astype(jnp.bfloat16)
    q_width = q_weight.shape[2]
    summed = contract_with(normed, lax.all_gather(q_weight[0], "ctx", axis=0, tiled=True))
    queries = (summed * factor).astype(jnp.bfloat16)
    half = tok_rows // 2
    own_pos = base + jnp.arange(tok_rows, dtype=jnp.int32)
    blocks = (queries[:half], queries[half:])
    positions = (own_pos[:half], own_pos[half:])
    heads = q_width // head_size
    fresh = (
        jnp.full((heads, half), -1e30, jnp.float32),
        jnp.zeros((heads, half), jnp.float32),
        jnp.zeros((half, heads, head_size), jnp.float32),
    )
    carry = (fresh, fresh)
    piece = lax.all_gather(shared, "ctx", axis=0, tiled=True)
    start = jnp.int32(0)
    results = []
    for block, spots, state in zip(blocks, positions, carry):

        def apply(current, block=block, spots=spots):
            return online_step(current, block, spots, piece)

        def keep(current):
            return current

        results.append(lax.cond(start <= spots[-1], apply, keep, state))
    states = tuple(results)
    finished = [
        (accum / total.T[:, :, None]).reshape(half, q_width).astype(jnp.bfloat16)
        for top, total, accum in states
    ]
    cross = jnp.concatenate([finished[0], finished[1]], axis=0)
    projected = rows_times(cross, lax.all_gather(out_weight[0], "ctx", axis=1, tiled=True))
    return (projected.astype(jnp.bfloat16)[None], shared)


def solution(mesh):
    return jax.shard_map(
        per_device,
        mesh=mesh,
        in_specs=(
            P("section", "ctx", None),
            P("ctx", None),
            P("ctx", None),
            P(None, ("section", "ctx")),
            P(("section", "ctx"), None),
            P("section", "ctx", None),
            P("section", None, "ctx"),
        ),
        out_specs=(P("section", "ctx", None), P("ctx", None)),
        check_vma=False,
    )
```

profile of v0, /device:TPU:6, one launch (start us, length us, event | category | flops | bytes accessed | tf_op | source)
XLA Modules:
  0.0 1056.3 jit_solution(15588916122435036196)
XLA Ops:
  8.0 0.7 all-gather.16.cloned.1.call-update
  9.4 1.9 collective-permute-start
  11.5 8.4 collective-permute-done
  20.0 0.9 constant_dynamic-update-slice_fusion
  21.4 402.7 %all-gather.18.cloned.1.call-done = bf16[256,20,256]{2,1,0:T(8,128)(2,1)} async-done(((bf16[1,20,256]{2,1,0:T(8,128)(2,1)}), bf16[256,20,256]{2,1,0:T(8,128)(2,1)}) %all-gather.18.cloned.1.call-update) | async-done | bytes 2621456 | tf_op jit(solution)/shard_map/all_gather | solution.py:90
  424.1 3.6 reshape.188
  427.7 415.4 %all-gather.16.cloned.1.call-done = bf16[256,20,640]{2,1,0:T(8,128)(2,1)} async-done(((bf16[1,20,640]{2,1,0:T(8,128)(2,1)}), bf16[256,20,640]{2,1,0:T(8,128)(2,1)}) %all-gather.16.cloned.1.call-update) | async-done | bytes 6553616 | tf_op jit(solution)/shard_map/all_gather | solution.py:86
  843.1 10.6 %reshape.186 = bf16[5120,640]{1,0:T(8,128)(2,1)} reshape(bf16[256,20,640]{2,1,0:T(8,128)(2,1)} %all-gather.16.cloned.1.call-done) | data formatting | bytes 13107200
  853.7 5.1 multiply_reduce_fusion
  859.3 30.2 %all_gather.20 = bf16[192,256]{1,0:T(8,128)(2,1)} all-gather(bf16[24,256]{1,0:T(8,128)(2,1)S(1)} %fusion.80), channel_id=1, replica_groups=mesh['section'=8,'ctx'=32] {'section'}, dimensions={0}, use_global_device_ids=true | all-gather | bytes 110592 | tf_op jit(solution)/shard_map/all_gather | solution.py:92
  892.0 2.0 fusion.57
  894.1 20.6 %all-gather.12.cloned.1.call-done = bf16[1,5120,640]{2,1,0:T(8,128)(2,1)} async-done(((bf16[1,160,640]{2,1,0:T(8,128)(2,1)}), bf16[1,5120,640]{2,1,0:T(8,128)(2,1)}) %all-gather.12.cloned.1.call-update) | async-done | bytes 6553616 | tf_op jit(solution)/shard_map/all_gather | solution.py:99
  914.7 5.2 fusion.67
  919.9 51.0 %all-gather.10.cloned.1.call-done = bf16[6144,256]{1,0:T(8,128)(2,1)} async-done(((bf16[192,256]{1,0:T(8,128)(2,1)}), bf16[6144,256]{1,0:T(8,128)(2,1)}) %all-gather.10.cloned.1.call-update) | async-done | bytes 3145744 | tf_op jit(solution)/shard_map/all_gather | solution.py:112
  970.9 10.5 conditional.2
  971.6 3.4 fusion
  975.0 3.2 fusion.16
  978.3 3.2 fusion.2
  981.7 10.9 %conditional.3 = (f32[5,96]{1,0:T(8,128)S(1)}, f32[96,5,128]{2,0,1:T(8,128)S(1)}) conditional(s32[]{:T(128)} %bitcast.26, () %tuple.26, (s32[192]{0:T(256)S(1)}, bf16[6144,256]{1,0:T(8,128)(2,1)}, bf16[192,640]{1,0:T(8,128)(2,1)S(1)}) %tuple.28), branch_computations={%region_8.9_spmd, %region_9.12_spmd} | conditional | flops 1540092288 | bytes 54604204 | solution.py:123
  982.8 3.5 fusion.23
  986.3 3.2 fusion.39
  989.5 3.2 fusion.25
  993.0 49.3 %all-gather.14.cloned.1.call-done = bf16[1,640,5120]{1,2,0:T(8,128)(2,1)} async-done(((bf16[1,640,160]{1,2,0:T(8,128)(2,1)}), bf16[1,640,5120]{1,2,0:T(8,128)(2,1)}) %all-gather.14.cloned.1.call-update) | async-done | bytes 6553616 | tf_op jit(solution)/shard_map/all_gather | solution.py:130
  1042.3 6.8 fusion.54
  (46 shorter events, 6.5 us)
Async XLA Ops:
  7.2 13.7 %copy-start = (bf16[192,640]{1,0:T(8,128)(2,1)S(1)}, bf16[192,640]{1,0:T(8,128)(2,1)}, u32[]{:S(2)}) copy-start(bf16[192,640]{1,0:T(8,128)(2,1)} %param.12) | copy-start | bytes 737284
  7.2 416.9 %all-gather.18.cloned.1.call-start = ((), (), s32[]{:S(2)}) async-start(), calls=%async_computation.4 | async-start | bytes 3158016 | tf_op jit(solution)/shard_map/all_gather | solution.py:90
  7.9 835.2 %all-gather.16.cloned.1.call-start = ((), (), s32[]{:S(2)}) async-start(), calls=%async_computation.3 | async-start | bytes 7895040 | tf_op jit(solution)/shard_map/all_gather | solution.py:86
  8.7 906.0 %all-gather.12.cloned.1.call-start = ((), (), s32[]{:S(2)}) async-start(), calls=%async_computation.1 | async-start | bytes 6758400 | tf_op jit(solution)/shard_map/all_gather | solution.py:99
  9.4 961.5 %all-gather.10.cloned.1.call-start = ((), (), s32[]{:S(2)}) async-start(), calls=%async_computation | async-start | bytes 3244032 | tf_op jit(solution)/shard_map/all_gather | solution.py:112
  9.4 10.5 collective-permute-start
  889.5 152.8 %all-gather.14.cloned.1.call-start = ((), (), s32[]{:S(2)}) async-start(), calls=%async_computation.2 | async-start | bytes 6758400 | tf_op jit(solution)/shard_map/all_gather | solution.py:130
  971.6 3.5 copy-start.2
  982.8 3.5 copy-start.3
  1042.3 7.5 copy-start.1
  1042.3 6.8 copy-start.4
Sparse Core Ops, SparseCore 0:
  9.9 414.1 all-gather.17
  426.0 417.0 all-gather.15
  845.6 68.9 all-gather.11
  917.1 53.8 all-gather.9
  973.3 68.9 all-gather.13
where the time goes:
time: 1060 us
  waiting for transfers between devices  950 us (90%)
  matrix products  31.5 us (3%)
  blocking collectives  30.2 us (3%)
  local copies, waits for them, and re-layouts  17.3 us (2%)
  between operations  15.2 us (1%)
    all_gather x1, waiting for transfers between devices, per_device(): lax.all_gather(self_out_weight, ('section', 'ctx'), axis=1, tiled=True)  415 us
    all_gather x1, waiting for transfers between devices, per_device(): lax.all_gather(kv_weight, ('section', 'ctx'), axis=0, tiled=True)  403 us
    all_gather x1, waiting for transfers between devices, per_device(): piece = lax.all_gather(shared, 'ctx', axis=0, tiled=True)  51 us
    all_gather x1, waiting for transfers between devices, per_device(): lax.all_gather(out_weight[0], 'ctx', axis=1, tiled=True)  49.3 us
    all_gather x1, blocking collectives, per_device(): shared = lax.all_gather(part_rows, 'section', axis=0, tiled=True)  30.2 us
  transfers between devices with their start and end apart: 6, of which 6 were waited for; matrix products, arithmetic and copies ran while one was open for 5% of the time, Pallas kernels for 0%

commit v1 on v0

v1 whole, which is shorter than its diff:
```python
import functools
import math

import jax
import jax.numpy as jnp
from jax import lax
from jax.experimental import pallas as pl
from jax.experimental.pallas import tpu as pltpu
from jax.sharding import PartitionSpec as P

MESH = pl.DeviceIdType.MESH
WINDOW = 128
F32 = jnp.float32
BF16 = jnp.bfloat16
NEG = -1e30

NT = (((1,), (1,)), ((), ()))
NN = (((1,), (0,)), ((), ()))

SELF_ROWS = 32
PART = 48


def dot(a, b, dims=NN):
    return lax.dot_general(a, b, dims, preferred_element_type=F32)


class Place:
    def __init__(self):
        section = lax.axis_index("section")
        ctx = lax.axis_index("ctx")
        self.at = dict(zl=section // 4, y=section % 4, x=ctx // 8, zh=(ctx // 2) % 4, co=ctx % 2)
        self.ctx = ctx
        self.section = section

    SIZE = dict(zl=2, y=4, x=4, zh=4, co=2)

    def shifted(self, axis, step):
        size = self.SIZE[axis]
        return lax.rem(self.at[axis] + (step + size), size)

    def device(self, **steps):
        c = dict(self.at)
        for axis, step in steps.items():
            c[axis] = self.shifted(axis, step)
        return (c["zl"] * 4 + c["y"], (c["x"] * 4 + c["zh"]) * 2 + c["co"])

    def ctx_device(self, step):
        return (self.section, lax.rem(self.ctx + step + 32, 32))


class Copies:
    def __init__(self, send, recv):
        self.send, self.recv = send, recv
        self.count = 0
        self.open = []

    def remote(self, src, dst, device):
        i = self.count
        self.count += 1
        copy = pltpu.make_async_remote_copy(
            src_ref=src, dst_ref=dst, send_sem=self.send.at[i], recv_sem=self.recv.at[i],
            device_id=device, device_id_type=MESH)
        copy.start()
        self.open.append(copy)
        return copy

    def local(self, src, dst):
        i = self.count
        self.count += 1
        copy = pltpu.make_async_copy(src, dst, self.send.at[i])
        copy.start()
        return copy

    def drain(self):
        for copy in self.open:
            copy.wait_send()


class Gather:
    def __init__(self, place, copies, buf, low, cut, high, first, second):
        self.place, self.copies, self.buf = place, copies, buf
        self.low, self.cut, self.high = low, cut, high
        self.first, self.second = first, second
        self.got = {}
        self.swaps = {}

    def block(self, i, j, low, high):
        x, zh = (i, j) if self.first == "x" else (j, i)
        index = self.place.shifted("x", x) * 4 + self.place.shifted("zh", zh)
        return self.buf.at[index, self.place.at["co"], pl.ds(low, high - low)]

    def put(self, key, i, j, low, high, axis, step):
        ref = self.block(i, j, low, high)
        self.got[key] = self.copies.remote(ref, ref, self.place.device(**{axis: step}))

    def start1(self):
        self.put("p", 0, 0, self.low, self.high, self.first, 1)
        self.put("n", 0, 0, self.low, self.high, self.first, -1)

    def forward1(self):
        self.got["p"].wait_recv()
        self.put("fp", -1, 0, self.low, self.cut, self.first, 1)
        self.got["n"].wait_recv()
        self.put("fn", 1, 0, self.cut, self.high, self.first, -1)

    def start2(self, i):
        if i == 2:
            self.got["fp"].wait_recv()
            self.got["fn"].wait_recv()
        self.put(("p", i), i, 0, self.low, self.high, self.second, 1)
        self.put(("n", i), i, 0, self.low, self.high, self.second, -1)

    def forward2(self, i):
        self.got["p", i].wait_recv()
        self.put(("fp", i), i, -1, self.low, self.cut, self.second, 1)
        self.got["n", i].wait_recv()
        self.put(("fn", i), i, 1, self.cut, self.high, self.second, -1)

    def finish2(self, i):
        self.got["fp", i].wait_recv()
        self.got["fn", i].wait_recv()

    def swap(self, x):
        ref = self.buf.at[pl.ds(self.place.shifted("x", x) * 4, 4), self.place.at["co"],
                          pl.ds(self.low, self.high - self.low)]
        self.swaps[x] = self.copies.remote(ref, ref, self.place.device(co=1))

    def swapped(self, x):
        self.swaps[x].wait_recv()


def eye_rows(rows, columns):
    return lax.broadcasted_iota(jnp.int32, (rows, columns), 0) == lax.broadcasted_iota(jnp.int32, (rows, columns), 1)


def kernel(x_in, q_in, kv_in, so_in, kw_in, wq_in, wo_in, out, shared,
           xv, normed, wq, wo, sw, near, kv, stage, gathered, window, qacc, queries, top, total, accum, cross, res,
           send, recv):
    place = Place()
    copies = Copies(send, recv)
    ctx = place.ctx
    at = place.at
    me = at["x"] * 4 + at["zh"]
    core = at["co"]
    rows = q_in.shape[0]
    heads = q_in.shape[1] // 128
    factor = 1.0 / math.sqrt(128)

    friends = [place.device(x=1), place.device(x=-1), place.device(x=2), place.device(zh=1), place.device(zh=-1),
               place.device(zh=2), place.device(co=1), place.ctx_device(1), place.ctx_device(-1)]
    for zl in (0, 1):
        for y in range(4):
            if zl or y:
                friends.append(place.device(zl=zl, y=y))
    barrier = pltpu.get_barrier_semaphore()
    for friend in friends:
        pl.semaphore_signal(barrier, inc=1, device_id=friend, device_id_type=MESH)

    x_copy = copies.local(x_in.at[0], xv)
    wq_copy = copies.local(wq_in.at[0], wq.at[me, core])

    pick = eye_rows(SELF_ROWS, so_in.shape[1]).astype(BF16)
    sw[me, core, :, 0:640] = dot(pick, so_in[...], NT).astype(BF16)
    sw[me, core, :, 640:896] = dot(pick, kw_in[...], NN).astype(BF16)
    near[128:320, :] = kv_in[...]
    wq_copy.wait()
    pl.semaphore_wait(barrier, len(friends))

    gs = Gather(place, copies, sw, 0, 16, 32, "zh", "x")
    qa = Gather(place, copies, wq, 0, 64, 128, "zh", "x")
    qb = Gather(place, copies, wq, 128, 144, 160, "x", "zh")
    oa = Gather(place, copies, wo, 0, 64, 128, "zh", "x")
    ob = Gather(place, copies, wo, 128, 144, 160, "x", "zh")

    rim = copies.remote(kv_in.at[pl.ds(64, 128)], near.at[pl.ds(0, 128)], place.ctx_device(1))
    gs.start1()
    gs.start2(0)
    qb.start1()
    qa.start1()
    qa.start2(0)

    wo[me, core] = dot(eye_rows(160, 160).astype(BF16), wo_in[0], NT).astype(BF16)

    gs.forward1()
    gs.start2(-1)
    gs.start2(1)
    rim.wait_recv()

    qpos = lax.broadcasted_iota(jnp.int32, (rows, 320), 0)
    kpos = lax.broadcasted_iota(jnp.int32, (rows, 320), 1) - 128
    allowed = (kpos <= qpos) & (kpos > qpos - WINDOW) & (kpos >= -rows * ctx)
    for h in range(heads):
        scores = dot(q_in[:, h * 128:(h + 1) * 128], near[:, 0:128], NT) * factor
        scores = jnp.where(allowed, scores, NEG)
        expo = jnp.where(allowed, jnp.exp(scores - jnp.max(scores, axis=1, keepdims=True)), 0.0)
        numer = dot(expo.astype(BF16), near[:, 128:256])
        window[:, h * 128:(h + 1) * 128] = (numer / jnp.sum(expo, axis=1, keepdims=True)).astype(BF16)

    gs.start2(2)
    gs.swap(0)
    qb.forward1()
    qb.start2(0)
    gs.forward2(0)
    gs.forward2(-1)
    gs.forward2(1)
    qa.forward1()
    qa.start2(-1)
    qa.start2(1)
    gs.forward2(2)
    for i in (0, -1, 1, 2):
        gs.finish2(i)
    for x in (-1, 1, 2):
        gs.swap(x)
    qb.start2(-1)
    qb.start2(1)
    for x in (0, -1, 1, 2):
        gs.swapped(x)

    weights = sw[...].reshape(32 * SELF_ROWS, 896)
    mixed = dot(window[...], weights[:, 0:640], NT).astype(BF16)
    wide = mixed.astype(F32)
    squares = jnp.sum(wide * wide, axis=1, keepdims=True)
    raw = dot(mixed, weights[:, 640:896])
    diagonal = eye_rows(PART, 128)
    for s in range(8):
        y, half = s % 4, s // 4
        stage[s, 0:PART] = raw[y * PART:(y + 1) * PART, half * 128:(half + 1) * 128]
        line = jnp.sum(jnp.where(diagonal, squares[y * PART:(y + 1) * PART], 0.0), axis=0, keepdims=True)
        stage[s, PART:PART + 8] = jnp.broadcast_to(line, (8, 128))
    mine = place.section
    reduces = []
    for zl in (0, 1):
        for y in range(4):
            if zl or y:
                to = place.device(zl=zl, y=y)
                reduces.append((copies.remote(stage.at[to[0]], gathered.at[zl * 4 + y - 1], to)))

    qb.start2(2)
    qa.forward2(0)
    qa.start2(2)

    x_copy.wait()

    def norm_rows(i, carry):
        block = pl.ds(pl.multiple_of(i * 16, 16), 16)
        hidden = xv[block, :].astype(F32)
        scale = lax.rsqrt(jnp.sum(hidden * hidden, axis=1, keepdims=True) / hidden.shape[1] + 1e-6)
        hidden = (hidden * scale).astype(BF16)
        for g in range(4):
            normed[g, block, :] = hidden[:, g * 1280:(g + 1) * 1280]
        return carry

    lax.fori_loop(0, rows // 16, norm_rows, 0)

    for r in reduces:
        r.wait_recv()
    summed = stage[mine]
    for slot in range(7):
        summed = summed + gathered[slot]
    column = jnp.sum(jnp.where(diagonal, summed[PART:PART + 1], 0.0), axis=1, keepdims=True)
    piece = (summed[0:PART] * lax.rsqrt(column / 5120.0 + 1e-6)).astype(BF16)
    half, y = at["zl"], at["y"]
    kv[half, y, core, me] = piece

    own = kv.at[half, y, core, me]
    first = [copies.remote(own, own, place.device(zh=k)) for k in (1, -1, 2)]
    qa.forward2(-1)
    qb.forward2(0)
    for c in first:
        c.wait_recv()
    own = kv.at[half, y, core, pl.ds(at["x"] * 4, 4)]
    second = [copies.remote(own, own, place.device(x=k)) for k in (1, -1, 2)]
    qa.forward2(1)
    qa.swap(0)
    oa.start1()
    ob.start1()
    qb.forward2(-1)
    qb.forward2(1)
    for c in second:
        c.wait_recv()
    own = kv.at[half, y, core]
    across = copies.remote(own, own, place.device(zl=1))
    ring = {k: copies.remote(own, own, place.device(y=k)) for k in (1, -1, 2)}
    sibling = [copies.remote(own, own, place.device(co=1))]
    qa.forward2(2)
    qb.forward2(2)
    oa.start2(0)
    other = lax.rem(half + 1, 2)
    across.wait_recv()
    theirs = kv.at[other, y, core]
    ring2 = {k: copies.remote(theirs, theirs, place.device(y=k)) for k in (1, -1, 2)}
    sibling.append(copies.remote(theirs, theirs, place.device(co=1)))
    oa.forward1()
    oa.start2(-1)
    oa.start2(1)
    ob.forward1()
    ob.start2(0)
    for i in (0, -1, 1, 2):
        qa.finish2(i)
        qb.finish2(i)
    for x in (-1, 1, 2):
        qa.swap(x)
    for x in (0, -1, 1, 2):
        qb.swap(x)

    for n, x in enumerate((0, -1, 1, 2)):
        qa.swapped(x)
        qb.swapped(x)
        where = place.shifted("x", x)
        product = dot(normed[where], wq[pl.ds(where * 4, 4)].reshape(1280, 640))
        if n == 0:
            qacc[...] = product
        else:
            qacc[...] += product
    scaled = (qacc[...] * factor).astype(BF16)
    for h in range(heads):
        queries[h] = scaled[:, h * 128:(h + 1) * 128]

    top[...] = jnp.full_like(top, NEG)
    total[...] = jnp.zeros_like(total)
    accum[...] = jnp.zeros_like(accum)
    ob.start2(-1)
    ob.start2(1)
    oa.forward2(0)
    oa.start2(2)
    ob.start2(2)

    def attend(part):
        def step(n, carry):
            c, chips = n // 2, (n % 2) * 8
            first_ctx = chips * 2 + c
            last_ctx = first_ctx + 14

            def update(masked):
                block = pl.ds(pl.multiple_of(chips, 8), 8)
                keys = kv[0, part, c, block].reshape(8 * PART, 128)
                values = kv[1, part, c, block].reshape(8 * PART, 128)
                if masked:
                    lane = lax.broadcasted_iota(jnp.int32, (1, 8 * PART), 1)
                    chip = jnp.zeros_like(lane)
                    for k in range(1, 8):
                        chip = chip + (lane >= k * PART).astype(jnp.int32)
                    position = (first_ctx + 2 * chip) * 192 + part * PART + lane - chip * PART
                    row = lax.broadcasted_iota(jnp.int32, (rows, 1), 0) + ctx * rows
                    ok = position <= row
                for h in range(heads):
                    scores = dot(queries[h], keys, NT)
                    if masked:
                        scores = jnp.where(ok, scores, NEG)
                    old = top[h]
                    new = jnp.maximum(old, jnp.max(scores, axis=1, keepdims=True))
                    expo = jnp.exp(scores - new)
                    if masked:
                        expo = jnp.where(ok, expo, 0.0)
                    fade = jnp.exp(old - new)
                    total[h] = total[h] * fade + jnp.sum(expo, axis=1, keepdims=True)
                    accum[h] = accum[h] * fade + dot(expo.astype(BF16), values)
                    top[h] = new

            @pl.when(last_ctx < ctx)
            def _():
                update(False)

            @pl.when((first_ctx <= ctx) & (last_ctx >= ctx))
            def _():
                update(True)

            return carry

        lax.fori_loop(0, 4, step, 0)

    for c in sibling:
        c.wait_recv()
    attend(y)
    oa.forward2(-1)
    ob.forward2(0)
    for n, k in enumerate((1, -1, 2)):
        part = place.shifted("y", -k)
        ring[k].wait_recv()
        ring2[k].wait_recv()
        ref = kv.at[half, part, core]
        a = copies.remote(ref, ref, place.device(co=1))
        ref = kv.at[other, part, core]
        b = copies.remote(ref, ref, place.device(co=1))
        if n == 0:
            oa.forward2(1)
            ob.forward2(-1)
        elif n == 1:
            oa.forward2(2)
            ob.forward2(1)
        else:
            ob.forward2(2)
        a.wait_recv()
        b.wait_recv()
        attend(part)
    oa.swap(0)

    for k in range(4):
        shared[k * PART:(k + 1) * PART, 0:128] = kv[0, k, core, me]
        shared[k * PART:(k + 1) * PART, 128:256] = kv[1, k, core, me]
    for h in range(heads):
        cross[:, h * 128:(h + 1) * 128] = (accum[h] / total[h]).astype(BF16)

    for i in (0, -1, 1, 2):
        oa.finish2(i)
        ob.finish2(i)
    for x in (-1, 1, 2):
        oa.swap(x)
    for x in (0, -1, 1, 2):
        ob.swap(x)

    writes = []
    for n, x in enumerate((0, -1, 1, 2)):
        oa.swapped(x)
        ob.swapped(x)
        where = place.shifted("x", x)
        for pair in range(2):
            w = wo[pl.ds(where * 4 + 2 * pair, 2)].reshape(640, 640)
            res[n * 2 + pair] = dot(cross[...], w, NT).astype(BF16)
            columns = pl.ds(pl.multiple_of((where * 2 + pair) * 640, 640), 640)
            writes.append(copies.local(res.at[n * 2 + pair], out.at[0, :, columns]))
    for w in writes:
        w.wait()
    copies.drain()


COPIES = 288


def per_device(layer_input, self_q, self_kv, self_out_weight, kv_weight, q_weight, out_weight):
    vmem = pl.BlockSpec(memory_space=pltpu.VMEM)
    hbm = pl.BlockSpec(memory_space=pl.ANY)
    tokens = self_q.shape[0]
    return pl.pallas_call(
        kernel,
        name="layer_group",
        out_shape=(jax.ShapeDtypeStruct((1, tokens, 5120), BF16), jax.ShapeDtypeStruct((tokens, 256), BF16)),
        in_specs=[hbm, vmem, vmem, vmem, vmem, hbm, vmem],
        out_specs=(hbm, vmem),
        scratch_shapes=[
            pltpu.VMEM((tokens, 5120), BF16),
            pltpu.VMEM((4, tokens, 1280), BF16),
            pltpu.VMEM((16, 2, 160, 640), BF16),
            pltpu.VMEM((16, 2, 160, 640), BF16),
            pltpu.VMEM((16, 2, SELF_ROWS, 896), BF16),
            pltpu.VMEM((320, 256), BF16),
            pltpu.VMEM((2, 4, 2, 16, PART, 128), BF16),
            pltpu.VMEM((8, PART + 8, 128), F32),
            pltpu.VMEM((7, PART + 8, 128), F32),
            pltpu.VMEM((tokens, 640), BF16),
            pltpu.VMEM((tokens, 640), F32),
            pltpu.VMEM((5, tokens, 128), BF16),
            pltpu.VMEM((5, tokens, 1), F32),
            pltpu.VMEM((5, tokens, 1), F32),
            pltpu.VMEM((5, tokens, 128), F32),
            pltpu.VMEM((tokens, 640), BF16),
            pltpu.VMEM((8, tokens, 640), BF16),
            pltpu.SemaphoreType.DMA((COPIES,)),
            pltpu.SemaphoreType.DMA((COPIES,)),
        ],
        compiler_params=pltpu.CompilerParams(
            collective_id=0, has_side_effects=True, vmem_limit_bytes=56 << 20),
    )(layer_input, self_q, self_kv, self_out_weight, kv_weight, q_weight, out_weight)


def solution(mesh):
    return jax.shard_map(
        per_device,
        mesh=mesh,
        in_specs=(
            P("section", "ctx", None),
            P("ctx", None),
            P("ctx", None),
            P(None, ("section", "ctx")),
            P(("section", "ctx"), None),
            P("section", "ctx", None),
            P("section", None, "ctx"),
        ),
        out_specs=(P("section", "ctx", None), P("ctx", None)),
        check_vma=False,
    )
```

time: 1060 us -> 136 us (0.13)
  waiting for transfers between devices: 950 us -> 0 us
  Pallas kernels: 0 us -> 128 us
  matrix products: 31.5 us -> 0 us
  blocking collectives: 30.2 us -> 0 us
  between operations: 15.2 us -> 0.65 us
    all_gather x5 -> x0, waiting for transfers between devices: 939 us -> none  [the longest x1 415 us: per_device(): lax.all_gather(self_out_weight, ('section', 'ctx'), axis=1, tiled=True)]
    pallas_call x0 -> x1, Pallas kernels: none -> 128 us  [per_device(): pl.pallas_call(kernel, name='layer_group', out_shape=(jax.ShapeDtypeStruc...]
    dot_general x9 -> x0, matrix products: 31.1 us -> none  [the longest x2 12 us: rows_times(): return jnp.dot(left, piece, preferred_element_type=jnp.float32)]
    all_gather x1 -> x0, blocking collectives: 30.2 us -> none  [per_device(): shared = lax.all_gather(part_rows, 'section', axis=0, tiled=True)]
  transfers between devices with their start and end apart: 6 -> 0, of which waited for: 6 -> 0; matrix products, arithmetic and copies ran while one was open for 5% -> 0% of each run, Pallas kernels for 0% -> 0%
where the time goes in v1:
time: 136 us; the launch traced here: 135 us
  Pallas kernels  128 us (94%)
  local copies, waits for them, and re-layouts  7.01 us (5%)
    pallas_call x1, Pallas kernels, per_device(): pl.pallas_call(kernel, name='layer_group', out_shape=(jax.ShapeDtypeStruc...  128 us
    unnamed x6, local copies, waits for them, and re-layouts  7.01 us

profile of v1, /device:TPU:6, one launch (start us, length us, event | category | flops | bytes accessed | tf_op | source)
XLA Modules:
  0.0 135.4 jit_solution(12060025779964633496)
XLA Ops:
  0.6 1.6 %copy.9.so_in = bf16[640,20]{1,0:T(8,128)(2,1)} copy(bf16[640,20]{0,1:T(8,128)(2,1)} %param.10) | data formatting | bytes 51200 | tf_op args[3]
  2.2 1.8 %copy.10.wo_in = bf16[1,640,160]{2,1,0:T(8,128)(2,1)} copy(bf16[1,640,160]{1,2,0:T(8,128)(2,1)} %param.13) | data formatting | bytes 409600 | tf_op args[6]
  4.0 127.7 %layer_group.1 = (bf16[1,192,5120]{2,1,0:T(8,128)(2,1)}, bf16[192,256]{1,0:T(8,128)(2,1)}) custom-call(bf16[1,192,5120]{2,1,0:T(8,128)(2,1)} %x_in.1, bf16[192,640]{1,0:T(8,128)(2,1)} %q_in.1, bf16[192,256]{1,0:T(8,128)(2,1)} %kv_in.1, bf16[640,20]{1,0:T(8,128)(2,1)} %copy.9.so_in, bf16[20,256]{1,0:T(8,128)(2,1)} %kw_in.1, bf16[1,160,640]{2,1,0:T(8,128)(2,1)} %wq_in.1, ...), custom_call_target="tpu_custom_call" | custom-call | tf_op jit(solution)/shard_map/layer_group/pallas_call | solution.py:435
  131.7 0.0 copy-start
  131.7 3.0 %copy.13 = bf16[1,192,5120]{2,1,0:T(8,128)(2,1)} copy(bf16[1,192,5120]{2,1,0:T(8,128)(2,1)} %get-tuple-element.4) | data formatting | bytes 3932160
  134.7 0.0 copy-done
  134.7 0.6 copy.14
Async XLA Ops:
  131.7 3.0 %copy-start = (bf16[192,256]{1,0:T(8,128)(2,1)S(1)}, bf16[192,256]{1,0:T(8,128)(2,1)}, u32[]{:S(2)}) copy-start(bf16[192,256]{1,0:T(8,128)(2,1)} %get-tuple-element.5) | copy-start | bytes 294916

commit v2 on v1

v2 whole, which is shorter than its diff:
```python
import functools
import math

import jax
import jax.numpy as jnp
from jax import lax
from jax.experimental import pallas as pl
from jax.experimental.pallas import tpu as pltpu
from jax.sharding import PartitionSpec as P

MESH = pl.DeviceIdType.MESH
WINDOW = 128
F32 = jnp.float32
BF16 = jnp.bfloat16
NEG = -1e30

NT = (((1,), (1,)), ((), ()))
NN = (((1,), (0,)), ((), ()))

SELF_ROWS = 32
PART = 48
LOW = -1e20


def dot(a, b, dims=NN):
    return lax.dot_general(a, b, dims, preferred_element_type=F32)


class Place:
    def __init__(self):
        section = lax.axis_index("section")
        ctx = lax.axis_index("ctx")
        self.at = dict(zl=section // 4, y=section % 4, x=ctx // 8, zh=(ctx // 2) % 4, co=ctx % 2)
        self.ctx = ctx
        self.section = section

    SIZE = dict(zl=2, y=4, x=4, zh=4, co=2)

    def shifted(self, axis, step):
        size = self.SIZE[axis]
        return lax.rem(self.at[axis] + (step + size), size)

    def device(self, **steps):
        c = dict(self.at)
        for axis, step in steps.items():
            c[axis] = self.shifted(axis, step)
        return (c["zl"] * 4 + c["y"], (c["x"] * 4 + c["zh"]) * 2 + c["co"])

    def ctx_device(self, step):
        return (self.section, lax.rem(self.ctx + step + 32, 32))


class Copies:
    def __init__(self, send, recv):
        self.send, self.recv = send, recv
        self.sends, self.recvs = {}, {}

    def index(self, table, name):
        return table.setdefault(name, len(table))

    def remote(self, ref, device, send, recv, dst=None):
        pltpu.make_async_remote_copy(
            src_ref=ref, dst_ref=ref if dst is None else dst,
            send_sem=self.send.at[self.index(self.sends, send)],
            recv_sem=self.recv.at[self.index(self.recvs, recv)],
            device_id=device, device_id_type=MESH).start()

    def local(self, src, dst, send):
        pltpu.make_async_copy(src, dst, self.send.at[self.index(self.sends, send)]).start()

    def arrived(self, recv, like):
        pltpu.make_async_copy(like, like, self.recv.at[self.recvs[recv]]).wait()

    def left(self, send, like):
        pltpu.make_async_copy(like, like, self.send.at[self.sends[send]]).wait()


class Gather:
    def __init__(self, name, place, copies, buf, low, cut, high, first, second):
        self.name, self.place, self.copies, self.buf = name, place, copies, buf
        self.low, self.cut, self.high = low, cut, high
        self.first, self.second = first, second

    def put(self, key, i, j, low, high, axis, step):
        x, zh = (i, j) if self.first == "x" else (j, i)
        index = self.place.shifted("x", x) * 4 + self.place.shifted("zh", zh)
        ref = self.buf.at[index, self.place.at["co"], pl.ds(low, high - low)]
        self.copies.remote(ref, self.place.device(**{axis: step}), self.name, (self.name, key))

    def like(self, blocks):
        return self.buf.at[pl.ds(0, blocks), 0, pl.ds(self.low, self.high - self.low)]

    def got(self, key, blocks):
        self.copies.arrived((self.name, key), self.like(blocks))

    def start1(self):
        self.put("near", 0, 0, self.low, self.high, self.first, 1)
        self.put("near", 0, 0, self.low, self.high, self.first, -1)

    def forward1(self):
        self.got("near", 2)
        self.put("far", -1, 0, self.low, self.cut, self.first, 1)
        self.put("far", 1, 0, self.cut, self.high, self.first, -1)

    def finish1(self):
        self.got("far", 1)

    def start2(self, i):
        self.put(("near", i), i, 0, self.low, self.high, self.second, 1)
        self.put(("near", i), i, 0, self.low, self.high, self.second, -1)

    def forward2(self, i):
        self.got(("near", i), 2)
        self.put(("far", i), i, -1, self.low, self.cut, self.second, 1)
        self.put(("far", i), i, 1, self.cut, self.high, self.second, -1)

    def finish2(self, i):
        self.got(("far", i), 1)

    def sent(self):
        self.copies.left(self.name, self.like(15))


def eye_rows(rows, columns):
    return lax.broadcasted_iota(jnp.int32, (rows, columns), 0) == lax.broadcasted_iota(jnp.int32, (rows, columns), 1)


def spread(column, width):
    return jnp.broadcast_to(column, (column.shape[0], width))


def kernel(x_in, q_in, kv_in, so_in, kw_in, wq_in, wo_in, out, shared,
           xv, normed, wq, wo, sz, sw, near, kv, stage, gathered, window, qacc, queries, top, accum, cross, res,
           send, recv):
    place = Place()
    copies = Copies(send, recv)
    ctx = place.ctx
    at = place.at
    me = at["x"] * 4 + at["zh"]
    core = at["co"]
    rows = q_in.shape[0]
    heads = q_in.shape[1] // 128
    factor = 1.0 / math.sqrt(128)
    sibling = place.device(co=1)
    columns = so_in.shape[0]

    friends = [place.device(x=1), place.device(x=-1), place.device(x=2), place.device(zh=1), place.device(zh=-1),
               place.device(zh=2), sibling, place.ctx_device(1), place.ctx_device(-1)]
    for zl in (0, 1):
        for y in range(4):
            if zl or y:
                friends.append(place.device(zl=zl, y=y))
    barrier = pltpu.get_barrier_semaphore()
    for friend in friends:
        pl.semaphore_signal(barrier, inc=1, device_id=friend, device_id_type=MESH)

    copies.local(wq_in.at[0], wq.at[me, core], "wq in")
    copies.local(x_in.at[0], xv, "x in")
    copies.local(wo_in, wo.at[me, core], "wo in")

    sz[at["zh"]] = jnp.zeros((SELF_ROWS, 896), BF16)
    sz[at["zh"], 0:columns, 0:640] = so_in[...]
    sz[at["zh"], 0:columns, 640:896] = kw_in[...]
    near[128:320, :] = kv_in[...]
    copies.left("wq in", wq.at[me, core])
    pl.semaphore_wait(barrier, len(friends))

    qa = Gather("qa", place, copies, wq, 0, 64, 128, "zh", "x")
    qb = Gather("qb", place, copies, wq, 128, 144, 160, "x", "zh")
    oa = Gather("oa", place, copies, wo, 0, 64, 128, "zh", "x")
    ob = Gather("ob", place, copies, wo, 128, 144, 160, "x", "zh")

    def swap(name, buf, x):
        copies.remote(buf.at[pl.ds(place.shifted("x", x) * 4, 4), core], sibling, name + " swap", (name, "swap", x))

    def swapped(name, buf, x):
        copies.arrived((name, "swap", x), buf.at[pl.ds(0, 4), 0])

    for k in (1, -1, 2):
        copies.remote(sz.at[at["zh"]], place.device(zh=k), "self z", "self z")
    copies.remote(kv_in.at[pl.ds(64, 128)], place.ctx_device(1), "rim", "rim", near.at[pl.ds(0, 128)])
    qb.start1()
    qa.start2(0)
    qa.start1()
    copies.arrived("rim", near.at[pl.ds(0, 128)])

    qpos = lax.broadcasted_iota(jnp.int32, (rows, 320), 0)
    kpos = lax.broadcasted_iota(jnp.int32, (rows, 320), 1) - 128
    allowed = (kpos <= qpos) & (kpos > qpos - WINDOW) & (kpos >= -rows * ctx)
    for h in range(heads):
        scores = dot(q_in[:, h * 128:(h + 1) * 128], near[:, 0:128], NT) * factor
        scores = jnp.where(allowed, scores, NEG)
        expo = jnp.exp(scores - jnp.max(scores, axis=1, keepdims=True))
        numer = dot(expo.astype(BF16), near[:, 128:256])
        window[:, h * 128:(h + 1) * 128] = (numer / jnp.sum(expo, axis=1, keepdims=True)).astype(BF16)

    copies.arrived("self z", sz.at[pl.ds(0, 3)])
    for k in range(4):
        sw[at["x"], core, k * columns:(k + 1) * columns, :] = sz[k, 0:columns, :]
    own = sw.at[at["x"], core]
    for k in (1, -1, 2):
        copies.remote(own, place.device(x=k), "self x", "self x")
    copies.remote(own, sibling, "self swap", "self swap")
    qb.forward1()
    qa.forward2(0)
    qb.start2(0)

    copies.left("x in", xv)

    def norm_rows(i, carry):
        block = pl.ds(pl.multiple_of(i * 16, 16), 16)
        hidden = xv[block, :].astype(F32)
        scale = lax.rsqrt(jnp.sum(hidden * hidden, axis=1, keepdims=True) / hidden.shape[1] + 1e-6)
        hidden = (hidden * scale).astype(BF16)
        for g in range(4):
            normed[g, block, :] = hidden[:, g * 1280:(g + 1) * 1280]
        return carry

    lax.fori_loop(0, rows // 16, norm_rows, 0)

    qa.forward1()
    qa.start2(-1)
    copies.arrived("self x", sw.at[pl.ds(0, 3), 0])
    for k in (1, -1, 2):
        copies.remote(sw.at[place.shifted("x", k), core], sibling, "self swap", "self swap")
    qb.start2(-1)
    copies.arrived("self swap", sw.at[:, 0])

    weights = sw[...].reshape(32 * columns, 896)
    mixed = dot(window[...], weights[:, 0:640], NT).astype(BF16)
    wide = mixed.astype(F32)
    squares = jnp.sum(wide * wide, axis=1, keepdims=True)
    raw = dot(mixed, weights[:, 640:896])
    diagonal = eye_rows(PART, 128)
    for s in range(8):
        y, half = s % 4, s // 4
        stage[s, 0:PART] = raw[y * PART:(y + 1) * PART, half * 128:(half + 1) * 128]
        line = jnp.sum(jnp.where(diagonal, squares[y * PART:(y + 1) * PART], 0.0), axis=0, keepdims=True)
        stage[s, PART:PART + 8] = jnp.broadcast_to(line, (8, 128))
    for zl in (0, 1):
        for y in range(4):
            if zl or y:
                to = place.device(zl=zl, y=y)
                copies.remote(stage.at[to[0]], to, "reduce", "reduce", gathered.at[zl * 4 + y - 1])

    qa.start2(1)
    qa.finish1()
    qb.start2(1)
    qa.forward2(-1)
    copies.arrived("reduce", gathered)
    summed = stage[place.section]
    for slot in range(7):
        summed = summed + gathered[slot]
    column = jnp.sum(jnp.where(diagonal, summed[PART:PART + 1], 0.0), axis=1, keepdims=True)
    half, y = at["zl"], at["y"]
    other = lax.rem(half + 1, 2)

    def group(h, part, c):
        return (h * 4 + part) * 2 + c

    mine = group(half, y, core)
    kv[mine, me] = (summed[0:PART] * lax.rsqrt(column / 5120.0 + 1e-6)).astype(BF16)

    for k in (1, -1, 2):
        copies.remote(kv.at[mine, me], place.device(zh=k), "kv piece", "kv z")
    qb.finish1()
    qb.start2(2)
    qb.forward2(0)
    copies.arrived("kv z", kv.at[0, pl.ds(0, 3)])
    for k in (1, -1, 2):
        copies.remote(kv.at[mine, pl.ds(at["x"] * 4, 4)], place.device(x=k), "kv piece", "kv x")
    qa.start2(2)
    qb.forward2(-1)
    copies.left("wo in", wo.at[me, core])
    ob.start1()
    copies.arrived("kv x", kv.at[0, pl.ds(0, 12)])

    def round_start(h):
        for k in (1, -1):
            copies.remote(kv.at[group(h, y, core)], place.device(y=k), "kv group", ("kv near", h is half))

    def round_forward(h):
        copies.arrived(("kv near", h is half), kv.at[pl.ds(0, 2)])
        copies.remote(kv.at[group(h, place.shifted("y", -1), core), pl.ds(0, 8)], place.device(y=1),
                      "kv group", ("kv far", h is half))
        copies.remote(kv.at[group(h, place.shifted("y", 1), core), pl.ds(8, 8)], place.device(y=-1),
                      "kv group", ("kv far", h is half))

    def hand(h, part, name):
        copies.remote(kv.at[group(h, part, core)], sibling, "kv swap", name)

    copies.remote(kv.at[mine], place.device(zl=1), "kv group", "kv across")
    round_start(half)
    hand(half, y, "kv swap 0")
    qa.forward2(1)
    qb.forward2(1)
    oa.start1()
    qa.forward2(2)
    qb.forward2(2)
    copies.arrived("kv across", kv.at[0])
    round_start(other)
    hand(other, y, "kv swap 0")
    oa.start2(0)
    round_forward(half)
    ob.forward1()

    top[...] = jnp.full_like(top, LOW)
    accum[...] = jnp.zeros_like(accum)

    for n, x in enumerate((0, -1, 1, 2)):
        qa.finish2(x)
    for x in (0, -1, 1, 2):
        qb.finish2(x)
    for x in (0, -1, 1, 2):
        swap("wq", wq, x)
    ob.start2(0)

    for n, x in enumerate((0, -1, 1, 2)):
        swapped("wq", wq, x)
        where = place.shifted("x", x)
        product = dot(normed[where], wq[pl.ds(where * 4, 4)].reshape(1280, 640))
        if n == 0:
            qacc[...] = product
        else:
            qacc[...] += product
    scaled = (qacc[...] * factor).astype(BF16)
    for h in range(heads):
        queries[h] = scaled[:, h * 128:(h + 1) * 128]

    lane = lax.broadcasted_iota(jnp.int32, (1, 16 * PART), 1)
    chip = jnp.zeros_like(lane)
    for k in range(1, 16):
        chip = chip + (lane >= k * PART).astype(jnp.int32)
    position0 = chip * (2 * rows) + lane - chip * PART
    row = lax.broadcasted_iota(jnp.int32, (rows, 1), 0) + ctx * rows
    ones = jnp.ones((16 * PART, 128), BF16)

    def attend(part, c):
        keys = kv[group(0, part, c)].reshape(16 * PART, 128)
        values = kv[group(1, part, c)].reshape(16 * PART, 128)
        both = jnp.concatenate([values, ones], axis=1)
        bias = jnp.where(position0 + (c * rows + part * PART) <= row, 0.0, NEG)
        for h in range(heads):
            scores = dot(queries[h], keys, NT) + bias
            old = top[h]
            new = jnp.maximum(old, spread(jnp.max(scores, axis=1, keepdims=True), 128))
            expo = jnp.exp(scores - jnp.tile(new, (1, 6)))
            fade = jnp.exp(old - new)
            accum[h] = accum[h] * jnp.tile(fade, (1, 2)) + dot(expo.astype(BF16), both)
            top[h] = new

    oa.forward1()
    oa.start2(-1)
    copies.arrived("kv swap 0", kv.at[pl.ds(0, 2)])
    attend(y, 0)
    round_forward(other)
    for h in (half, other):
        for k in (1, -1):
            hand(h, place.shifted("y", k), "kv swap 1")
    oa.start2(1)
    oa.forward2(0)
    oa.finish1()
    ob.start2(-1)
    attend(y, 1)
    oa.start2(2)
    ob.finish1()
    ob.start2(1)
    ob.start2(2)
    copies.arrived("kv swap 1", kv.at[pl.ds(0, 4)])
    attend(place.shifted("y", -1), 0)
    ob.forward2(0)
    oa.forward2(-1)
    attend(place.shifted("y", -1), 1)
    for h in (half, other):
        copies.arrived(("kv far", h is half), kv.at[0])
        hand(h, place.shifted("y", 2), "kv swap 2")
    ob.forward2(-1)
    attend(place.shifted("y", 1), 0)
    oa.forward2(1)
    ob.forward2(1)
    attend(place.shifted("y", 1), 1)
    copies.arrived("kv swap 2", kv.at[pl.ds(0, 2)])
    ob.forward2(2)
    attend(place.shifted("y", 2), 0)
    oa.forward2(2)
    attend(place.shifted("y", 2), 1)

    for h in range(heads):
        cross[:, h * 128:(h + 1) * 128] = (accum[h, :, 0:128] / accum[h, :, 128:256]).astype(BF16)
    for k in range(4):
        shared[k * PART:(k + 1) * PART, 0:128] = kv[group(0, k, core), me]
        shared[k * PART:(k + 1) * PART, 128:256] = kv[group(1, k, core), me]

    for x in (0, -1, 1, 2):
        ob.finish2(x)
    for x in (0, -1, 1, 2):
        oa.finish2(x)
        swap("wo", wo, x)
    for n, x in enumerate((0, -1, 1, 2)):
        swapped("wo", wo, x)
        where = place.shifted("x", x)
        for pair in range(2):
            w = wo[pl.ds(where * 4 + 2 * pair, 2)].reshape(640, 640)
            res[n * 2 + pair] = dot(cross[...], w, NT).astype(BF16)
            block = pl.ds(pl.multiple_of((where * 2 + pair) * 640, 640), 640)
            copies.local(res.at[n * 2 + pair], out.at[0, :, block], "out")

    for gather in (qa, qb, oa, ob):
        gather.sent()
    copies.left("wq swap", wq.at[:, 0])
    copies.left("wo swap", wo.at[:, 0])
    copies.left("self z", sz.at[pl.ds(0, 3)])
    copies.left("self x", sw.at[pl.ds(0, 3), 0])
    copies.left("self swap", sw.at[:, 0])
    copies.left("rim", near.at[pl.ds(0, 128)])
    copies.left("reduce", gathered)
    copies.left("kv piece", kv.at[0, pl.ds(0, 15)])
    copies.left("kv group", kv.at[pl.ds(0, 7)])
    copies.left("kv swap", kv.at[pl.ds(0, 8)])
    copies.left("out", res)
    assert (len(copies.sends), len(copies.recvs)) == (SENDS, RECVS), (len(copies.sends), len(copies.recvs))


SENDS = 18
RECVS = 63


def per_device(layer_input, self_q, self_kv, self_out_weight, kv_weight, q_weight, out_weight):
    vmem = pl.BlockSpec(memory_space=pltpu.VMEM)
    hbm = pl.BlockSpec(memory_space=pl.ANY)
    tokens = self_q.shape[0]
    columns = kv_weight.shape[0]
    return pl.pallas_call(
        kernel,
        name="layer_group",
        out_shape=(jax.ShapeDtypeStruct((1, tokens, 5120), BF16), jax.ShapeDtypeStruct((tokens, 256), BF16)),
        in_specs=[hbm, vmem, vmem, vmem, vmem, hbm, hbm],
        out_specs=(hbm, vmem),
        scratch_shapes=[
            pltpu.VMEM((tokens, 5120), BF16),
            pltpu.VMEM((4, tokens, 1280), BF16),
            pltpu.VMEM((16, 2, 160, 640), BF16),
            pltpu.VMEM((16, 2, 160, 640), BF16),
            pltpu.VMEM((4, SELF_ROWS, 896), BF16),
            pltpu.VMEM((4, 2, 4 * columns, 896), BF16),
            pltpu.VMEM((320, 256), BF16),
            pltpu.VMEM((16, 16, PART, 128), BF16),
            pltpu.VMEM((8, PART + 8, 128), F32),
            pltpu.VMEM((7, PART + 8, 128), F32),
            pltpu.VMEM((tokens, 640), BF16),
            pltpu.VMEM((tokens, 640), F32),
            pltpu.VMEM((5, tokens, 128), BF16),
            pltpu.VMEM((5, tokens, 128), F32),
            pltpu.VMEM((5, tokens, 256), F32),
            pltpu.VMEM((tokens, 640), BF16),
            pltpu.VMEM((8, tokens, 640), BF16),
            pltpu.SemaphoreType.DMA((SENDS,)),
            pltpu.SemaphoreType.DMA((RECVS,)),
        ],
        compiler_params=pltpu.CompilerParams(
            collective_id=0, has_side_effects=True, vmem_limit_bytes=56 << 20),
    )(layer_input, self_q, self_kv, self_out_weight.T, kv_weight, q_weight, out_weight[0].T)


def solution(mesh):
    return jax.shard_map(
        per_device,
        mesh=mesh,
        in_specs=(
            P("section", "ctx", None),
            P("ctx", None),
            P("ctx", None),
            P(None, ("section", "ctx")),
            P(("section", "ctx"), None),
            P("section", "ctx", None),
            P("section", None, "ctx"),
        ),
        out_specs=(P("section", "ctx", None), P("ctx", None)),
        check_vma=False,
    )
```

time: 136 us -> 99.1 us (0.73)
  Pallas kernels: 128 us -> 93.3 us
  local copies, waits for them, and re-layouts: 7.01 us -> 3.62 us
    pallas_call x1, Pallas kernels: 128 us -> 93.3 us  [per_device(): pl.pallas_call(kernel, name='layer_group', out_shape=(jax.ShapeDtypeStruc...]
    unnamed x6 -> x4, local copies, waits for them, and re-layouts: 7.01 us -> 3.62 us
where the time goes in v2:
time: 99.1 us; the launch traced here: 97.5 us
  Pallas kernels  93.3 us (94%)
  local copies, waits for them, and re-layouts  3.62 us (4%)
    pallas_call x1, Pallas kernels, per_device(): pl.pallas_call(kernel, name='layer_group', out_shape=(jax.ShapeDtypeStruc...  93.3 us
    unnamed x4, local copies, waits for them, and re-layouts  3.62 us

profile of v2, /device:TPU:6, one launch (start us, length us, event | category | flops | bytes accessed | tf_op | source)
XLA Modules:
  0.0 97.5 jit_solution(3209433923136993212)
XLA Ops:
  0.6 93.3 %layer_group.1 = (bf16[1,192,5120]{2,1,0:T(8,128)(2,1)}, bf16[192,256]{1,0:T(8,128)(2,1)}) custom-call(bf16[1,192,5120]{2,1,0:T(8,128)(2,1)} %x_in.1, bf16[192,640]{1,0:T(8,128)(2,1)} %q_in.1, bf16[192,256]{1,0:T(8,128)(2,1)} %kv_in.1, bf16[20,640]{1,0:T(8,128)(2,1)} %bitcast.5, bf16[20,256]{1,0:T(8,128)(2,1)} %kw_in.1, bf16[1,160,640]{2,1,0:T(8,128)(2,1)} %wq_in.1, ...), custom_call_target="tpu_custom_call" | custom-call | tf_op jit(solution)/shard_map/layer_group/pallas_call | solution.py:433
  93.9 0.0 copy-start
  93.9 3.0 %copy.11 = bf16[1,192,5120]{2,1,0:T(8,128)(2,1)} copy(bf16[1,192,5120]{2,1,0:T(8,128)(2,1)} %get-tuple-element.4) | data formatting | bytes 3932160
  96.9 0.0 copy-done
  96.9 0.6 copy.12
Async XLA Ops:
  93.9 3.0 %copy-start = (bf16[192,256]{1,0:T(8,128)(2,1)S(1)}, bf16[192,256]{1,0:T(8,128)(2,1)}, u32[]{:S(2)}) copy-start(bf16[192,256]{1,0:T(8,128)(2,1)} %get-tuple-element.5) | copy-start | bytes 294916

commit v3 on v2

v3 whole, which is shorter than its diff:
```python
import functools
import math

import jax
import jax.numpy as jnp
from jax import lax
from jax.experimental import pallas as pl
from jax.experimental.pallas import tpu as pltpu
from jax.sharding import PartitionSpec as P

MESH = pl.DeviceIdType.MESH
WINDOW = 128
F32 = jnp.float32
BF16 = jnp.bfloat16
NEG = -1e30

NT = (((1,), (1,)), ((), ()))
NN = (((1,), (0,)), ((), ()))

SELF_ROWS = 32
PART = 48
LOW = -1e20


def dot(a, b, dims=NN):
    return lax.dot_general(a, b, dims, preferred_element_type=F32)


class Place:
    def __init__(self):
        section = lax.axis_index("section")
        ctx = lax.axis_index("ctx")
        self.at = dict(zl=section // 4, y=section % 4, x=ctx // 8, zh=(ctx // 2) % 4, co=ctx % 2)
        self.ctx = ctx
        self.section = section

    SIZE = dict(zl=2, y=4, x=4, zh=4, co=2)

    def shifted(self, axis, step):
        size = self.SIZE[axis]
        return lax.rem(self.at[axis] + (step + size), size)

    def device(self, **steps):
        c = dict(self.at)
        for axis, step in steps.items():
            c[axis] = self.shifted(axis, step)
        return (c["zl"] * 4 + c["y"], (c["x"] * 4 + c["zh"]) * 2 + c["co"])

    def ctx_device(self, step):
        return (self.section, lax.rem(self.ctx + step + 32, 32))


class Copies:
    def __init__(self, send, recv):
        self.send, self.recv = send, recv
        self.sends, self.recvs = {}, {}

    def index(self, table, name):
        return table.setdefault(name, len(table))

    def remote(self, ref, device, send, recv, dst=None):
        pltpu.make_async_remote_copy(
            src_ref=ref, dst_ref=ref if dst is None else dst,
            send_sem=self.send.at[self.index(self.sends, send)],
            recv_sem=self.recv.at[self.index(self.recvs, recv)],
            device_id=device, device_id_type=MESH).start()

    def local(self, src, dst, send):
        pltpu.make_async_copy(src, dst, self.send.at[self.index(self.sends, send)]).start()

    def arrived(self, recv, like):
        pltpu.make_async_copy(like, like, self.recv.at[self.recvs[recv]]).wait()

    def left(self, send, like):
        pltpu.make_async_copy(like, like, self.send.at[self.sends[send]]).wait()


class Gather:
    def __init__(self, name, place, copies, buf, low, cut, high, first, second):
        self.name, self.place, self.copies, self.buf = name, place, copies, buf
        self.low, self.cut, self.high = low, cut, high
        self.first, self.second = first, second

    def put(self, key, i, j, low, high, axis, step):
        x, zh = (i, j) if self.first == "x" else (j, i)
        index = self.place.shifted("x", x) * 4 + self.place.shifted("zh", zh)
        ref = self.buf.at[index, self.place.at["co"], pl.ds(low, high - low)]
        self.copies.remote(ref, self.place.device(**{axis: step}), self.name, (self.name, key))

    def like(self, blocks):
        return self.buf.at[pl.ds(0, blocks), 0, pl.ds(self.low, self.high - self.low)]

    def got(self, key, blocks):
        self.copies.arrived((self.name, key), self.like(blocks))

    def start1(self):
        self.put("near", 0, 0, self.low, self.high, self.first, 1)
        self.put("near", 0, 0, self.low, self.high, self.first, -1)

    def forward1(self):
        self.got("near", 2)
        self.put("far", -1, 0, self.low, self.cut, self.first, 1)
        self.put("far", 1, 0, self.cut, self.high, self.first, -1)

    def start2(self, i):
        if i == 2:
            self.got("far", 1)
        self.put(("near", i), i, 0, self.low, self.high, self.second, 1)
        self.put(("near", i), i, 0, self.low, self.high, self.second, -1)

    def forward2(self, i):
        self.got(("near", i), 2)
        self.put(("far", i), i, -1, self.low, self.cut, self.second, 1)
        self.put(("far", i), i, 1, self.cut, self.high, self.second, -1)

    def finish2(self, i):
        self.got(("far", i), 1)

    def sent(self):
        self.copies.left(self.name, self.like(15))


class Swap:
    def __init__(self, name, place, copies, buf):
        self.name, self.place, self.copies, self.buf = name, place, copies, buf

    def put(self, x, ref):
        self.copies.remote(ref, self.place.device(co=1), (self.name, "swap"), (self.name, "swap", x))

    def rows(self, x, low, count):
        return self.buf.at[pl.ds(self.place.shifted("x", x) * 4, 4), self.place.at["co"], pl.ds(low, count)]

    def most(self, x):
        self.put(x, self.rows(x, 0, 128))

    def far(self, i):
        index = self.place.shifted("x", 2) * 4 + self.place.shifted("zh", i)
        self.put(2, self.buf.at[index, self.place.at["co"], pl.ds(0, 128)])

    def rest(self, x):
        self.put(x, self.rows(x, 128, 32))

    def done(self, x):
        self.copies.arrived((self.name, "swap", x), self.buf.at[pl.ds(0, 4), 0])


def eye_rows(rows, columns):
    return lax.broadcasted_iota(jnp.int32, (rows, columns), 0) == lax.broadcasted_iota(jnp.int32, (rows, columns), 1)


def spread(column, width):
    return jnp.broadcast_to(column, (column.shape[0], width))


def kernel(x_in, q_hbm, kv_in, so_hbm, kw_hbm, wq_in, wo_in, out, shared,
           q_in, so_in, kw_in, xv, normed, wq, wo, sz, sw, near, kv, stage, gathered, window, qacc, queries, top, accum, cross, res,
           send, recv):
    place = Place()
    copies = Copies(send, recv)
    ctx = place.ctx
    at = place.at
    me = at["x"] * 4 + at["zh"]
    core = at["co"]
    rows = q_in.shape[0]
    heads = q_in.shape[1] // 128
    factor = 1.0 / math.sqrt(128)
    sibling = place.device(co=1)
    columns = so_in.shape[0]

    friends = [place.device(x=1), place.device(x=-1), place.device(x=2), place.device(zh=1), place.device(zh=-1),
               place.device(zh=2), sibling, place.ctx_device(1), place.ctx_device(-1)]
    for zl in (0, 1):
        for y in range(4):
            if zl or y:
                friends.append(place.device(zl=zl, y=y))
    barrier = pltpu.get_barrier_semaphore()
    for friend in friends:
        pl.semaphore_signal(barrier, inc=1, device_id=friend, device_id_type=MESH)

    copies.local(so_hbm, so_in, "so in")
    copies.local(kw_hbm, kw_in, "kw in")
    copies.local(kv_in, near.at[pl.ds(128, rows)], "kv in")
    copies.local(wq_in.at[0], wq.at[me, core], "wq in")
    copies.local(q_hbm, q_in, "q in")
    copies.local(x_in.at[0], xv, "x in")
    copies.local(wo_in, wo.at[me, core], "wo in")

    sz[at["zh"]] = jnp.zeros((SELF_ROWS, 896), BF16)
    copies.left("so in", so_in)
    copies.left("kw in", kw_in)
    sz[at["zh"], 0:columns, 0:640] = so_in[...]
    sz[at["zh"], 0:columns, 640:896] = kw_in[...]
    copies.left("kv in", near.at[pl.ds(128, rows)])
    copies.left("wq in", wq.at[me, core])
    pl.semaphore_wait(barrier, len(friends))

    qa = Gather("qa", place, copies, wq, 0, 64, 128, "zh", "x")
    qb = Gather("qb", place, copies, wq, 128, 144, 160, "x", "zh")
    oa = Gather("oa", place, copies, wo, 0, 64, 128, "zh", "x")
    ob = Gather("ob", place, copies, wo, 128, 144, 160, "x", "zh")
    half, y = at["zl"], at["y"]
    other = lax.rem(half + 1, 2)
    diagonal = eye_rows(PART, 128)

    def group(h, part, c):
        return (h * 4 + part) * 2 + c

    mine = group(half, y, core)

    q_swap = Swap("wq", place, copies, wq)
    o_swap = Swap("wo", place, copies, wo)

    def start():
        for k in (1, -1, 2):
            copies.remote(sz.at[at["zh"]], place.device(zh=k), "self z", "self z")
        copies.remote(near.at[pl.ds(192, 128)], place.ctx_device(1), "rim", "rim", near.at[pl.ds(0, 128)])

    def window_attention():
        copies.left("q in", q_in)
        copies.arrived("rim", near.at[pl.ds(0, 128)])
        qpos = lax.broadcasted_iota(jnp.int32, (rows, 320), 0)
        kpos = lax.broadcasted_iota(jnp.int32, (rows, 320), 1) - 128
        allowed = (kpos <= qpos) & (kpos > qpos - WINDOW) & (kpos >= -rows * ctx)
        for h in range(heads):
            scores = dot(q_in[:, h * 128:(h + 1) * 128], near[:, 0:128], NT) * factor
            scores = jnp.where(allowed, scores, NEG)
            expo = jnp.exp(scores - jnp.max(scores, axis=1, keepdims=True))
            numer = dot(expo.astype(BF16), near[:, 128:256])
            window[:, h * 128:(h + 1) * 128] = (numer / jnp.sum(expo, axis=1, keepdims=True)).astype(BF16)

    def self_x():
        copies.arrived("self z", sz.at[pl.ds(0, 3)])
        for k in range(4):
            sw[at["x"], core, k * columns:(k + 1) * columns, :] = sz[k, 0:columns, :]
        own = sw.at[at["x"], core]
        for k in (1, -1, 2):
            copies.remote(own, place.device(x=k), "self x", "self x")
        copies.remote(own, sibling, "self swap", "self swap")

    def self_swap():
        copies.arrived("self x", sw.at[pl.ds(0, 3), 0])
        for k in (1, -1, 2):
            copies.remote(sw.at[place.shifted("x", k), core], sibling, "self swap", "self swap")

    def mix():
        copies.arrived("self swap", sw.at[:, 0])
        weights = sw[...].reshape(32 * columns, 896)
        mixed = dot(window[...], weights[:, 0:640], NT).astype(BF16)
        wide = mixed.astype(F32)
        squares = jnp.sum(wide * wide, axis=1, keepdims=True)
        raw = dot(mixed, weights[:, 640:896])
        for s in range(8):
            part, side = s % 4, s // 4
            stage[s, 0:PART] = raw[part * PART:(part + 1) * PART, side * 128:(side + 1) * 128]
            line = jnp.sum(jnp.where(diagonal, squares[part * PART:(part + 1) * PART], 0.0), axis=0, keepdims=True)
            stage[s, PART:PART + 8] = jnp.broadcast_to(line, (8, 128))
        for zl in (0, 1):
            for k in range(4):
                if zl or k:
                    to = place.device(zl=zl, y=k)
                    copies.remote(stage.at[to[0]], to, "reduce", "reduce", gathered.at[zl * 4 + k - 1])

    def reduce():
        copies.arrived("reduce", gathered)
        summed = stage[place.section]
        for slot in range(7):
            summed = summed + gathered[slot]
        column = jnp.sum(jnp.where(diagonal, summed[PART:PART + 1], 0.0), axis=1, keepdims=True)
        kv[mine, me] = (summed[0:PART] * lax.rsqrt(column / 5120.0 + 1e-6)).astype(BF16)
        for k in (1, -1, 2):
            copies.remote(kv.at[mine, me], place.device(zh=k), "kv piece", "kv z")

    def kv_x():
        copies.arrived("kv z", kv.at[0, pl.ds(0, 3)])
        for k in (1, -1, 2):
            copies.remote(kv.at[mine, pl.ds(at["x"] * 4, 4)], place.device(x=k), "kv piece", "kv x")

    def round_start(h):
        for k in (1, -1):
            copies.remote(kv.at[group(h, y, core)], place.device(y=k), "kv group", ("kv near", h is half))

    def hand(h, part, batch):
        copies.remote(kv.at[group(h, part, core)], sibling, "kv swap", ("kv swap", batch))

    def kv_round():
        copies.arrived("kv x", kv.at[0, pl.ds(0, 12)])
        copies.remote(kv.at[mine], place.device(zl=1), "kv group", "kv across")
        round_start(half)
        hand(half, y, 0)

    def kv_across():
        copies.arrived("kv across", kv.at[0])
        round_start(other)
        hand(other, y, 0)

    def round_forward(h):
        copies.arrived(("kv near", h is half), kv.at[pl.ds(0, 2)])
        copies.remote(kv.at[group(h, place.shifted("y", -1), core), pl.ds(0, 8)], place.device(y=1),
                      "kv group", ("kv far", h is half))
        copies.remote(kv.at[group(h, place.shifted("y", 1), core), pl.ds(8, 8)], place.device(y=-1),
                      "kv group", ("kv far", h is half))
        for k in (1, -1):
            hand(h, place.shifted("y", k), 1)

    def round_end(h):
        copies.arrived(("kv far", h is half), kv.at[0])
        hand(h, place.shifted("y", 2), 2)

    def normalise():
        copies.left("x in", xv)

        def norm_rows(i, carry):
            block = pl.ds(pl.multiple_of(i * 16, 16), 16)
            hidden = xv[block, :].astype(F32)
            scale = lax.rsqrt(jnp.sum(hidden * hidden, axis=1, keepdims=True) / hidden.shape[1] + 1e-6)
            hidden = (hidden * scale).astype(BF16)
            for g in range(4):
                normed[g, block, :] = hidden[:, g * 1280:(g + 1) * 1280]
            return carry

        lax.fori_loop(0, rows // 16, norm_rows, 0, unroll=3)

    seen = []

    def query_product(x):
        q_swap.done(x)
        where = place.shifted("x", x)
        product = dot(normed[where], wq[pl.ds(where * 4, 4)].reshape(1280, 640))
        if seen:
            qacc[...] += product
        else:
            qacc[...] = product
        seen.append(x)

    def finish_queries():
        scaled = (qacc[...] * factor).astype(BF16)
        for h in range(heads):
            queries[h] = scaled[:, h * 128:(h + 1) * 128]
        top[...] = jnp.full_like(top, LOW)
        accum[...] = jnp.zeros_like(accum)

    def handed(batch):
        copies.arrived(("kv swap", batch), kv.at[pl.ds(0, 4 if batch == 1 else 2)])

    def attend(k, c):
        part = place.shifted("y", k)
        lane = lax.broadcasted_iota(jnp.int32, (1, 16 * PART), 1)
        chip = jnp.zeros_like(lane)
        for n in range(1, 16):
            chip = chip + (lane >= n * PART).astype(jnp.int32)
        position = chip * (2 * rows - PART) + lane + (c * rows + part * PART)
        row = lax.broadcasted_iota(jnp.int32, (rows, 1), 0) + ctx * rows
        bias = jnp.where(position <= row, 0.0, NEG)
        keys = kv[group(0, part, c)].reshape(16 * PART, 128)
        values = kv[group(1, part, c)].reshape(16 * PART, 128)
        both = jnp.concatenate([values, jnp.ones((16 * PART, 128), BF16)], axis=1)
        for h in range(heads):
            scores = dot(queries[h], keys, NT) + bias
            old = top[h]
            new = jnp.maximum(old, spread(jnp.max(scores, axis=1, keepdims=True), 128))
            expo = jnp.exp(scores - jnp.tile(new, (1, 6)))
            fade = jnp.exp(old - new)
            accum[h] = accum[h] * jnp.tile(fade, (1, 2)) + dot(expo.astype(BF16), both)
            top[h] = new

    def finish_cross():
        for h in range(heads):
            cross[:, h * 128:(h + 1) * 128] = (accum[h, :, 0:128] / accum[h, :, 128:256]).astype(BF16)
        for k in range(4):
            shared[k * PART:(k + 1) * PART, 0:128] = kv[group(0, k, core), me]
            shared[k * PART:(k + 1) * PART, 128:256] = kv[group(1, k, core), me]

    def update(x):
        o_swap.done(x)
        where = place.shifted("x", x)
        for pair in range(2):
            w = wo[pl.ds(where * 4 + 2 * pair, 2)].reshape(640, 640)
            slot = (x % 4) * 2 + pair
            res[slot] = dot(cross[...], w, NT).astype(BF16)
            block = pl.ds(pl.multiple_of((where * 2 + pair) * 640, 640), 640)
            copies.local(res.at[slot], out.at[0, :, block], "out")

    start()
    copies.left("wo in", wo.at[me, core])
    oa.start2(0)
    qa.start2(0)
    qb.start1()
    normalise()
    ob.start1()
    qb.start2(0)
    oa.forward2(0)
    qa.start1()
    self_x()
    window_attention()
    qb.forward1()
    qa.forward2(0)
    ob.forward1()
    oa.finish2(0)
    o_swap.far(0)
    qb.forward2(0)
    qb.start2(1)
    qb.start2(-1)
    qa.forward1()
    qa.start2(1)
    qa.start2(-1)
    qb.finish2(0)
    q_swap.rest(0)
    self_swap()
    mix()
    qa.finish2(0)
    q_swap.far(0)
    qb.forward2(1)
    qb.forward2(-1)
    qb.start2(2)
    qa.forward2(1)
    reduce()
    qb.finish2(1)
    q_swap.rest(1)
    qa.start2(2)
    q_swap.most(0)
    qb.finish2(-1)
    q_swap.rest(-1)
    oa.start1()
    query_product(0)
    qa.finish2(1)
    q_swap.far(1)
    kv_x()
    qa.forward2(-1)
    qa.forward2(2)
    q_swap.most(-1)
    q_swap.most(1)
    qb.forward2(2)
    query_product(-1)
    kv_round()
    ob.start2(0)
    query_product(1)
    qa.finish2(-1)
    q_swap.far(-1)
    oa.forward1()
    oa.start2(1)
    oa.start2(-1)
    qb.finish2(2)
    q_swap.rest(2)
    qa.finish2(2)
    q_swap.far(2)
    query_product(2)
    finish_queries()
    kv_across()
    attend(0, core)
    handed(0)
    attend(0, 1 - core)
    round_forward(half)
    ob.start2(-1)
    ob.forward2(0)
    oa.forward2(1)
    ob.start2(1)
    oa.start2(2)
    o_swap.most(0)
    ob.start2(2)
    oa.forward2(-1)
    round_forward(other)
    attend(-1, core)
    ob.forward2(-1)
    handed(1)
    attend(-1, 1 - core)
    oa.finish2(1)
    ob.finish2(0)
    o_swap.far(1)
    round_end(half)
    o_swap.rest(0)
    attend(1, 1 - core)
    round_end(other)
    ob.forward2(1)
    attend(2, core)
    ob.forward2(2)
    oa.forward2(2)
    handed(2)
    attend(2, 1 - core)
    ob.finish2(-1)
    o_swap.rest(-1)
    o_swap.most(-1)
    o_swap.most(1)
    oa.finish2(-1)
    o_swap.far(-1)
    attend(1, core)
    ob.finish2(1)
    o_swap.rest(1)
    finish_cross()
    ob.finish2(2)
    o_swap.rest(2)
    update(0)
    oa.finish2(2)
    o_swap.far(2)
    update(-1)
    update(1)
    update(2)

    for gather in (qa, qb, oa, ob):
        gather.sent()
    copies.left(("wq", "swap"), wq.at[:, 0])
    copies.left(("wo", "swap"), wo.at[:, 0])
    copies.left("self z", sz.at[pl.ds(0, 3)])
    copies.left("self x", sw.at[pl.ds(0, 3), 0])
    copies.left("self swap", sw.at[:, 0])
    copies.left("rim", near.at[pl.ds(0, 128)])
    copies.left("reduce", gathered)
    copies.left("kv piece", kv.at[0, pl.ds(0, 15)])
    copies.left("kv group", kv.at[pl.ds(0, 7)])
    copies.left("kv swap", kv.at[pl.ds(0, 8)])
    copies.left("out", res)
    assert (len(copies.sends), len(copies.recvs)) == (SENDS, RECVS), (len(copies.sends), len(copies.recvs))


SENDS = 22
RECVS = 63


def per_device(layer_input, self_q, self_kv, self_out_weight, kv_weight, q_weight, out_weight):
    vmem = pl.BlockSpec(memory_space=pltpu.VMEM)
    hbm = pl.BlockSpec(memory_space=pltpu.HBM)
    free = pl.BlockSpec(memory_space=pl.ANY)
    tokens = self_q.shape[0]
    columns = kv_weight.shape[0]
    arrays = (layer_input, self_q, self_kv, self_out_weight.T, kv_weight, q_weight, out_weight[0].T)
    return pl.pallas_call(
        kernel,
        name="layer_group",
        out_shape=(jax.ShapeDtypeStruct((1, tokens, 5120), BF16), jax.ShapeDtypeStruct((tokens, 256), BF16)),
        in_specs=[hbm] * 7,
        out_specs=(free, vmem),
        scratch_shapes=[
            pltpu.VMEM((tokens, 640), BF16),
            pltpu.VMEM((columns, 640), BF16),
            pltpu.VMEM((columns, 256), BF16),
            pltpu.VMEM((tokens, 5120), BF16),
            pltpu.VMEM((4, tokens, 1280), BF16),
            pltpu.VMEM((16, 2, 160, 640), BF16),
            pltpu.VMEM((16, 2, 160, 640), BF16),
            pltpu.VMEM((4, SELF_ROWS, 896), BF16),
            pltpu.VMEM((4, 2, 4 * columns, 896), BF16),
            pltpu.VMEM((320, 256), BF16),
            pltpu.VMEM((16, 16, PART, 128), BF16),
            pltpu.VMEM((8, PART + 8, 128), F32),
            pltpu.VMEM((7, PART + 8, 128), F32),
            pltpu.VMEM((tokens, 640), BF16),
            pltpu.VMEM((tokens, 640), F32),
            pltpu.VMEM((5, tokens, 128), BF16),
            pltpu.VMEM((5, tokens, 128), F32),
            pltpu.VMEM((5, tokens, 256), F32),
            pltpu.VMEM((tokens, 640), BF16),
            pltpu.VMEM((8, tokens, 640), BF16),
            pltpu.SemaphoreType.DMA((SENDS,)),
            pltpu.SemaphoreType.DMA((RECVS,)),
        ],
        compiler_params=pltpu.CompilerParams(
            collective_id=0, has_side_effects=True, vmem_limit_bytes=36 << 20),
    )(*[pltpu.with_memory_space_constraint(array, pltpu.HBM) for array in arrays])


def solution(mesh):
    return jax.shard_map(
        per_device,
        mesh=mesh,
        in_specs=(
            P("section", "ctx", None),
            P("ctx", None),
            P("ctx", None),
            P(None, ("section", "ctx")),
            P(("section", "ctx"), None),
            P("section", "ctx", None),
            P("section", None, "ctx"),
        ),
        out_specs=(P("section", "ctx", None), P("ctx", None)),
        check_vma=False,
    )
```

time: 99.1 us -> 83.8 us (0.85); the launches traced: 97.5 us -> 83.6 us
  Pallas kernels: 93.3 us -> 81.1 us
  local copies, waits for them, and re-layouts: 3.62 us -> 1.91 us
    pallas_call x1, Pallas kernels: 93.3 us -> 81.1 us  [per_device(): pl.pallas_call(kernel, name='layer_group', out_shape=(jax.ShapeDtypeStruc...]
    unnamed x4 -> x2, local copies, waits for them, and re-layouts: 3.62 us -> 1.91 us
where the time goes in v3:
time: 83.8 us; the launch traced here: 83.6 us
  Pallas kernels  81.1 us (97%)
  local copies, waits for them, and re-layouts  1.91 us (2%)
    pallas_call x1, Pallas kernels, per_device(): pl.pallas_call(kernel, name='layer_group', out_shape=(jax.ShapeDtypeStruc...  81.1 us
    unnamed x2, local copies, waits for them, and re-layouts  1.91 us

profile of v3, /device:TPU:6, one launch (start us, length us, event | category | flops | bytes accessed | tf_op | source)
XLA Modules:
  0.0 83.6 jit_solution(17980829925681355511)
XLA Ops:
  0.6 81.1 %layer_group.1 = (bf16[1,192,5120]{2,1,0:T(8,128)(2,1)S(1)}, bf16[192,256]{1,0:T(8,128)(2,1)S(1)}) custom-call(bf16[1,192,5120]{2,1,0:T(8,128)(2,1)} %x_in.1, bf16[192,640]{1,0:T(8,128)(2,1)} %q_hbm.1, bf16[192,256]{1,0:T(8,128)(2,1)} %kv_in.1, bf16[20,640]{1,0:T(8,128)(2,1)} %bitcast.5, bf16[20,256]{1,0:T(8,128)(2,1)} %kw_hbm.1, ...), custom_call_target="tpu_custom_call" | custom-call | tf_op jit(solution)/shard_map/layer_group/pallas_call | solution.py:525
  81.7 1.3 %copy.11 = bf16[1,192,5120]{2,1,0:T(8,128)(2,1)} copy(bf16[1,192,5120]{2,1,0:T(8,128)(2,1)S(1)} %get-tuple-element.4) | data formatting | bytes 3932160
  83.0 0.6 copy.12

commit v4 on v3

--- a/solution.py
+++ b/solution.py
@@ -17,7 +17,6 @@
 NT = (((1,), (1,)), ((), ()))
 NN = (((1,), (0,)), ((), ()))
 
-SELF_ROWS = 32
 PART = 48
 LOW = -1e20
 
@@ -185,11 +184,13 @@
     copies.local(x_in.at[0], xv, "x in")
     copies.local(wo_in, wo.at[me, core], "wo in")
 
-    sz[at["zh"]] = jnp.zeros((SELF_ROWS, 896), BF16)
+    sz[at["zh"], 112:144, :] = jnp.zeros((32, 128), BF16)
     copies.left("so in", so_in)
     copies.left("kw in", kw_in)
-    sz[at["zh"], 0:columns, 0:640] = so_in[...]
-    sz[at["zh"], 0:columns, 640:896] = kw_in[...]
+    for n in range(7):
+        ref, lane = (so_in, n * 128) if n < 5 else (kw_in, (n - 5) * 128)
+        sz[at["zh"], 16 * n:16 * n + 16, :] = ref[0:16, lane:lane + 128]
+        sz[at["zh"], 112 + 4 * n:116 + 4 * n, :] = ref[16:20, lane:lane + 128]
     copies.left("kv in", near.at[pl.ds(128, rows)])
     copies.left("wq in", wq.at[me, core])
     pl.semaphore_wait(barrier, len(friends))
@@ -231,7 +232,10 @@
     def self_x():
         copies.arrived("self z", sz.at[pl.ds(0, 3)])
         for k in range(4):
-            sw[at["x"], core, k * columns:(k + 1) * columns, :] = sz[k, 0:columns, :]
+            for n in range(7):
+                lanes = slice(n * 128, n * 128 + 128)
+                sw[at["x"], core, k * 20:k * 20 + 16, lanes] = sz[k, 16 * n:16 * n + 16, :]
+                sw[at["x"], core, k * 20 + 16:k * 20 + 20, lanes] = sz[k, 112 + 4 * n:116 + 4 * n, :]
         own = sw.at[at["x"], core]
         for k in (1, -1, 2):
             copies.remote(own, place.device(x=k), "self x", "self x")
@@ -387,112 +391,112 @@
     qb.start1()
     normalise()
     ob.start1()
-    qb.start2(0)
-    oa.forward2(0)
     qa.start1()
     self_x()
+    oa.forward2(0)
     window_attention()
+    qa.forward2(0)
     qb.forward1()
-    qa.forward2(0)
+    qb.start2(-1)
     ob.forward1()
+    qb.start2(0)
+    qb.start2(1)
+    qb.forward2(-1)
+    qa.forward1()
+    self_swap()
+    qa.start2(-1)
+    qa.start2(1)
+    mix()
+    qb.finish2(-1)
+    q_swap.rest(-1)
     oa.finish2(0)
     o_swap.far(0)
-    qb.forward2(0)
-    qb.start2(1)
-    qb.start2(-1)
-    qa.forward1()
-    qa.start2(1)
-    qa.start2(-1)
-    qb.finish2(0)
-    q_swap.rest(0)
-    self_swap()
-    mix()
     qa.finish2(0)
     q_swap.far(0)
     qb.forward2(1)
-    qb.forward2(-1)
+    qb.forward2(0)
     qb.start2(2)
-    qa.forward2(1)
+    qa.start2(2)
+    q_swap.most(0)
     reduce()
     qb.finish2(1)
     q_swap.rest(1)
-    qa.start2(2)
-    q_swap.most(0)
-    qb.finish2(-1)
-    q_swap.rest(-1)
+    qb.finish2(0)
+    q_swap.rest(0)
     oa.start1()
     query_product(0)
-    qa.finish2(1)
-    q_swap.far(1)
+    qa.forward2(-1)
     kv_x()
-    qa.forward2(-1)
+    qa.forward2(1)
     qa.forward2(2)
     q_swap.most(-1)
     q_swap.most(1)
     qb.forward2(2)
+    qa.finish2(-1)
+    q_swap.far(-1)
     query_product(-1)
-    kv_round()
     ob.start2(0)
     query_product(1)
-    qa.finish2(-1)
-    q_swap.far(-1)
+    kv_round()
     oa.forward1()
+    oa.start2(-1)
     oa.start2(1)
-    oa.start2(-1)
     qb.finish2(2)
     q_swap.rest(2)
+    qa.finish2(1)
+    q_swap.far(1)
     qa.finish2(2)
     q_swap.far(2)
+    ob.start2(-1)
     query_product(2)
     finish_queries()
     kv_across()
     attend(0, core)
     handed(0)
     attend(0, 1 - core)
+    oa.forward2(-1)
     round_forward(half)
-    ob.start2(-1)
     ob.forward2(0)
-    oa.forward2(1)
-    ob.start2(1)
     oa.start2(2)
     o_swap.most(0)
+    ob.start2(1)
     ob.start2(2)
-    oa.forward2(-1)
+    oa.forward2(1)
+    ob.forward2(-1)
     round_forward(other)
-    attend(-1, core)
-    ob.forward2(-1)
+    attend(1, core)
+    ob.finish2(0)
+    o_swap.rest(0)
+    oa.finish2(-1)
+    o_swap.far(-1)
     handed(1)
     attend(-1, 1 - core)
-    oa.finish2(1)
-    ob.finish2(0)
-    o_swap.far(1)
+    ob.forward2(1)
     round_end(half)
-    o_swap.rest(0)
     attend(1, 1 - core)
     round_end(other)
-    ob.forward2(1)
-    attend(2, core)
     ob.forward2(2)
     oa.forward2(2)
+    ob.finish2(-1)
+    o_swap.rest(-1)
+    attend(2, core)
     handed(2)
     attend(2, 1 - core)
-    ob.finish2(-1)
-    o_swap.rest(-1)
-    o_swap.most(-1)
-    o_swap.most(1)
-    oa.finish2(-1)
-    o_swap.far(-1)
-    attend(1, core)
     ob.finish2(1)
     o_swap.rest(1)
-    finish_cross()
+    oa.finish2(1)
+    o_swap.far(1)
+    o_swap.most(1)
+    o_swap.most(-1)
+    attend(-1, core)
     ob.finish2(2)
     o_swap.rest(2)
+    finish_cross()
     update(0)
     oa.finish2(2)
     o_swap.far(2)
+    update(1)
     update(-1)
-    update(1)
     update(2)
 
     for gather in (qa, qb, oa, ob):
@@ -536,7 +540,7 @@
             pltpu.VMEM((4, tokens, 1280), BF16),
             pltpu.VMEM((16, 2, 160, 640), BF16),
             pltpu.VMEM((16, 2, 160, 640), BF16),
-            pltpu.VMEM((4, SELF_ROWS, 896), BF16),
+            pltpu.VMEM((4, 144, 128), BF16),
             pltpu.VMEM((4, 2, 4 * columns, 896), BF16),
             pltpu.VMEM((320, 256), BF16),
             pltpu.VMEM((16, 16, PART, 128), BF16),

time: 83.8 us -> 81.6 us (0.974); the launches traced: 83.6 us -> 80.5 us
  Pallas kernels: 81.1 us -> 77.9 us
    pallas_call x1, Pallas kernels: 81.1 us -> 77.9 us  [per_device(): pl.pallas_call(kernel, name='layer_group', out_shape=(jax.ShapeDtypeStruc...]
where the time goes in v4:
time: 81.6 us; the launch traced here: 80.5 us
  Pallas kernels  77.9 us (95%)
  local copies, waits for them, and re-layouts  1.91 us (2%)
    pallas_call x1, Pallas kernels, per_device(): pl.pallas_call(kernel, name='layer_group', out_shape=(jax.ShapeDtypeStruc...  77.9 us
    unnamed x2, local copies, waits for them, and re-layouts  1.91 us

profile of v4, /device:TPU:6, one launch (start us, length us, event | category | flops | bytes accessed | tf_op | source)
XLA Modules:
  0.0 80.5 jit_solution(6445007925512191190)
XLA Ops:
  0.6 77.9 %layer_group.1 = (bf16[1,192,5120]{2,1,0:T(8,128)(2,1)S(1)}, bf16[192,256]{1,0:T(8,128)(2,1)S(1)}) custom-call(bf16[1,192,5120]{2,1,0:T(8,128)(2,1)} %x_in.1, bf16[192,640]{1,0:T(8,128)(2,1)} %q_hbm.1, bf16[192,256]{1,0:T(8,128)(2,1)} %kv_in.1, bf16[20,640]{1,0:T(8,128)(2,1)} %bitcast.5, bf16[20,256]{1,0:T(8,128)(2,1)} %kw_hbm.1, ...), custom_call_target="tpu_custom_call" | custom-call | tf_op jit(solution)/shard_map/layer_group/pallas_call | solution.py:529
  78.6 1.3 %copy.11 = bf16[1,192,5120]{2,1,0:T(8,128)(2,1)} copy(bf16[1,192,5120]{2,1,0:T(8,128)(2,1)S(1)} %get-tuple-element.4) | data formatting | bytes 3932160
  79.8 0.6 copy.12

commit v5 on v4

--- a/solution.py
+++ b/solution.py
@@ -151,8 +151,8 @@
     return jnp.broadcast_to(column, (column.shape[0], width))
 
 
-def kernel(x_in, q_hbm, kv_in, so_hbm, kw_hbm, wq_in, wo_in, out, shared,
-           q_in, so_in, kw_in, xv, normed, wq, wo, sz, sw, near, kv, stage, gathered, window, qacc, queries, top, accum, cross, res,
+def kernel(x_in, q_hbm, kv_in, so_in, kw_in, wq_in, wo_in, out, shared,
+           q_in, xv, normed, wq, wo, sz, sw, near, kv, stage, gathered, window, qacc, queries, top, accum, cross, res,
            send, recv):
     place = Place()
     copies = Copies(send, recv)
@@ -176,8 +176,6 @@
     for friend in friends:
         pl.semaphore_signal(barrier, inc=1, device_id=friend, device_id_type=MESH)
 
-    copies.local(so_hbm, so_in, "so in")
-    copies.local(kw_hbm, kw_in, "kw in")
     copies.local(kv_in, near.at[pl.ds(128, rows)], "kv in")
     copies.local(wq_in.at[0], wq.at[me, core], "wq in")
     copies.local(q_hbm, q_in, "q in")
@@ -185,8 +183,6 @@
     copies.local(wo_in, wo.at[me, core], "wo in")
 
     sz[at["zh"], 112:144, :] = jnp.zeros((32, 128), BF16)
-    copies.left("so in", so_in)
-    copies.left("kw in", kw_in)
     for n in range(7):
         ref, lane = (so_in, n * 128) if n < 5 else (kw_in, (n - 5) * 128)
         sz[at["zh"], 16 * n:16 * n + 16, :] = ref[0:16, lane:lane + 128]
@@ -515,7 +511,7 @@
     assert (len(copies.sends), len(copies.recvs)) == (SENDS, RECVS), (len(copies.sends), len(copies.recvs))
 
 
-SENDS = 22
+SENDS = 20
 RECVS = 63
 
 
@@ -530,12 +526,10 @@
         kernel,
         name="layer_group",
         out_shape=(jax.ShapeDtypeStruct((1, tokens, 5120), BF16), jax.ShapeDtypeStruct((tokens, 256), BF16)),
-        in_specs=[hbm] * 7,
+        in_specs=[hbm, hbm, hbm, vmem, vmem, hbm, hbm],
         out_specs=(free, vmem),
         scratch_shapes=[
             pltpu.VMEM((tokens, 640), BF16),
-            pltpu.VMEM((columns, 640), BF16),
-            pltpu.VMEM((columns, 256), BF16),
             pltpu.VMEM((tokens, 5120), BF16),
             pltpu.VMEM((4, tokens, 1280), BF16),
             pltpu.VMEM((16, 2, 160, 640), BF16),

time: 81.6 us -> 82.2 us (level)
  no operation moved by 1% of the time
where the time goes in v5:
time: 82.2 us; the launch traced here: 80.8 us
  Pallas kernels  78.3 us (95%)
  local copies, waits for them, and re-layouts  1.91 us (2%)
    pallas_call x1, Pallas kernels, per_device(): pl.pallas_call(kernel, name='layer_group', out_shape=(jax.ShapeDtypeStruc...  78.3 us
    unnamed x2, local copies, waits for them, and re-layouts  1.91 us

profile of v5, /device:TPU:6, one launch (start us, length us, event | category | flops | bytes accessed | tf_op | source)
XLA Modules:
  0.0 80.8 jit_solution(1690576253658219575)
XLA Ops:
  0.6 78.3 %layer_group.1 = (bf16[1,192,5120]{2,1,0:T(8,128)(2,1)S(1)}, bf16[192,256]{1,0:T(8,128)(2,1)S(1)}) custom-call(bf16[1,192,5120]{2,1,0:T(8,128)(2,1)} %x_in.1, bf16[192,640]{1,0:T(8,128)(2,1)} %q_hbm.1, bf16[192,256]{1,0:T(8,128)(2,1)} %kv_in.1, bf16[20,640]{1,0:T(8,128)(2,1)} %bitcast.5, bf16[20,256]{1,0:T(8,128)(2,1)} %kw_in.1, bf16[1,160,640]{2,1,0:T(8,128)(2,1)} %wq_in.1, ...), custom_call_target="tpu_custom_call" | custom-call | tf_op jit(solution)/shard_map/layer_group/pallas_call | solution.py:525
  78.9 1.3 %copy.11 = bf16[1,192,5120]{2,1,0:T(8,128)(2,1)} copy(bf16[1,192,5120]{2,1,0:T(8,128)(2,1)S(1)} %get-tuple-element.4) | data formatting | bytes 3932160
  80.2 0.6 copy.12

commit v6 on v5

--- a/solution.py
+++ b/solution.py
@@ -385,9 +385,9 @@
     oa.start2(0)
     qa.start2(0)
     qb.start1()
-    normalise()
     ob.start1()
     qa.start1()
+    normalise()
     self_x()
     oa.forward2(0)
     window_attention()
@@ -489,9 +489,9 @@
     o_swap.rest(2)
     finish_cross()
     update(0)
+    update(1)
     oa.finish2(2)
     o_swap.far(2)
-    update(1)
     update(-1)
     update(2)
 

time: 82.2 us -> 82.5 us (level)
  no operation moved by 1% of the time
where the time goes in v6:
time: 82.5 us; the launch traced here: 81 us
  Pallas kernels  78.5 us (95%)
  local copies, waits for them, and re-layouts  1.91 us (2%)
    pallas_call x1, Pallas kernels, per_device(): pl.pallas_call(kernel, name='layer_group', out_shape=(jax.ShapeDtypeStruc...  78.5 us
    unnamed x2, local copies, waits for them, and re-layouts  1.91 us

profile of v6, /device:TPU:6, one launch (start us, length us, event | category | flops | bytes accessed | tf_op | source)
XLA Modules:
  0.0 81.0 jit_solution(7560725643999969891)
XLA Ops:
  0.6 78.5 %layer_group.1 = (bf16[1,192,5120]{2,1,0:T(8,128)(2,1)S(1)}, bf16[192,256]{1,0:T(8,128)(2,1)S(1)}) custom-call(bf16[1,192,5120]{2,1,0:T(8,128)(2,1)} %x_in.1, bf16[192,640]{1,0:T(8,128)(2,1)} %q_hbm.1, bf16[192,256]{1,0:T(8,128)(2,1)} %kv_in.1, bf16[20,640]{1,0:T(8,128)(2,1)} %bitcast.5, bf16[20,256]{1,0:T(8,128)(2,1)} %kw_in.1, bf16[1,160,640]{2,1,0:T(8,128)(2,1)} %wq_in.1, ...), custom_call_target="tpu_custom_call" | custom-call | tf_op jit(solution)/shard_map/layer_group/pallas_call | solution.py:525
  79.1 1.3 %copy.11 = bf16[1,192,5120]{2,1,0:T(8,128)(2,1)} copy(bf16[1,192,5120]{2,1,0:T(8,128)(2,1)S(1)} %get-tuple-element.4) | data formatting | bytes 3932160
  80.4 0.6 copy.12
